TPU v7x, 32 devices: a whole 2x2x4 slice. The times are simulated.
32 devices in a mesh: ctx: 8 (over z, x), head: 4 (over y, core).
Axes of the slice: x: 2, y: 2, z: 4, core: 2. Of those that a mesh axis runs over, the one named last changes fastest.
Arguments:
- queries: bfloat16 [2048, 4096], P('ctx', 'head'), may hold values from -64 to 64
- key_vectors: bfloat16 [2048, 1024], P('ctx', 'head'), may hold values from -4.5 to 4.5
- value_vectors: bfloat16 [2048, 1024], P('ctx', 'head'), may hold values from -6 to 6
- out_weight: bfloat16 [4096, 4096], P('head'), may hold values from -0.09375 to 0.09375
- offsets: int32 [5], replicated, may hold values from 0 to 2048, as said below
Outputs:
- projected: bfloat16 [4096, 2048], P('head', 'ctx')
Inputs may be any that keep to these rules, and one draw needn't show every extreme that they name: offsets[0] = 0 and offsets[4] = 2048; offsets rise strictly; every document has 1 to 1024 tokens and one has exactly 1024.
All inputs are finite; a program needn't handle non-finite values.
Results may differ from a plain program's by a relative error of at most 0.014.
Values may be sent and summed in bfloat16 or wider, within the bound.
No kernel may reach another device: no remote copies, remote signals or barrier semaphores. Data moves between devices by JAX's collectives and lax.ppermute only.
A program may use at most 64 MiB of HBM per device.

v0:
```python
import jax
import jax.numpy as jnp
from jax import lax
from jax.sharding import PartitionSpec as P

HEAD_DIM = 128
SPAN = 16


masked_score = -1e30


def shifted(block, axis, distance):
    devices = range(lax.axis_size(axis))
    route = [(i - distance, i) for i in devices if i - distance in devices]
    return lax.ppermute(block, axis, route)


def doc_index(positions, offsets):
    boundaries = offsets[1:-1]
    return jnp.sum((positions[:, None] >= boundaries[None, :]).astype(jnp.int32), axis=1)


def attend(running, query_head_rows, kv_block, key_start, query_pos, query_doc, offsets):
    key_count = kv_block.shape[1]
    kv_groups = query_head_rows.shape[1]
    head_size = query_head_rows.shape[3]
    logit_scale = head_size ** (-0.5)
    key_pos = key_start + jnp.arange(key_count, dtype=jnp.int32)
    key_doc = doc_index(key_pos, offsets)
    visible = (
        (key_pos[None, :] >= 0)
        & (key_pos[None, :] <= query_pos[:, None])
        & (key_doc[None, :] == query_doc[:, None])
    )
    row_max, row_sum, weighted_values = running
    grouped_key_heads = kv_block[0].reshape(key_count, kv_groups, head_size)
    value_heads = kv_block[1].reshape(key_count, kv_groups, head_size)
    attention_logits = (
        jnp.einsum(
            "myqe,cye->yqmc", query_head_rows, grouped_key_heads, preferred_element_type=jnp.float32
        )
        * logit_scale
    )
    attention_logits = jnp.where(visible, attention_logits, masked_score)
    new_max = jnp.maximum(row_max, jnp.max(attention_logits, axis=-1))
    attention_probs = jnp.where(visible, jnp.exp(attention_logits - new_max[..., None]), 0.0)
    rescale = jnp.exp(row_max - new_max)
    row_sum = row_sum * rescale + jnp.sum(attention_probs, axis=-1)
    added = jnp.einsum(
        "avmk,kab->mavb",
        attention_probs.astype(jnp.bfloat16),
        value_heads,
        preferred_element_type=jnp.float32,
    )
    weighted_values = weighted_values * jnp.transpose(rescale, (2, 0, 1))[..., None] + added
    return (new_max, row_sum, weighted_values)


def on_device(queries, key_vectors, value_vectors, out_weight, offsets):
    row_count = queries.shape[0]
    kv_groups = key_vectors.shape[1] // HEAD_DIM
    group_size = queries.shape[1] // key_vectors.shape[1]
    position = lax.axis_index("ctx")
    first_row = position * row_count
    query_pos = first_row + jnp.arange(row_count, dtype=jnp.int32)
    query_doc = doc_index(query_pos, offsets)
    query_head_rows = queries.reshape(row_count, kv_groups, group_size, HEAD_DIM)
    kv_pair = jnp.stack([key_vectors, value_vectors])
    empty_max = jnp.full((kv_groups, group_size, row_count), masked_score, jnp.float32)
    empty_sum = jnp.zeros((kv_groups, group_size, row_count), jnp.float32)
    empty_weighted = jnp.zeros((row_count, kv_groups, group_size, HEAD_DIM), jnp.float32)
    running = (empty_max, empty_sum, empty_weighted)
    reach_steps = min(SPAN - 1, lax.axis_size("ctx") - 1)
    running = attend(running, query_head_rows, kv_pair, first_row, query_pos, query_doc, offsets)

    def advance(step_index, current):
        totals, moving = current
        moving = shifted(moving, "ctx", 1)
        totals = attend(
            totals,
            query_head_rows,
            moving,
            first_row - step_index * row_count,
            query_pos,
            query_doc,
            offsets,
        )
        return (totals, moving)

    running, leftover = lax.fori_loop(1, reach_steps + 1, advance, (running, kv_pair))
    row_max, row_sum, weighted_values = running
    attended = weighted_values / jnp.transpose(row_sum, (2, 0, 1))[..., None]
    attended = attended.reshape(row_count, kv_groups * group_size * HEAD_DIM).astype(jnp.bfloat16)
    return lax.psum_scatter(
        lax.dot_general(
            out_weight, attended, (((0,), (1,)), ((), ())), preferred_element_type=jnp.float32
        ).astype(jnp.bfloat16),
        "head",
        scatter_dimension=0,
        tiled=True,
    )


def solution(mesh):
    placed = (P("ctx", "head"), P("ctx", "head"), P("ctx", "head"), P("head", None), P())
    return jax.shard_map(
        on_device, mesh=mesh, in_specs=placed, out_specs=P("head", "ctx"), check_vma=False
    )
```

profile of v0, /device:TPU:0, one launch (start us, length us, event | category | flops | bytes accessed | tf_op | source)
XLA Modules:
  0.0 158.4 jit_solution(15948300148655878542)
XLA Ops:
  6.5 0.9 reshape_squeeze_stack.6
  7.5 1.0 copy.32
  8.5 1.6 %reshape_squeeze_stack.7 = bf16[256,2,128]{2,1,0:T(2,128)(2,1)} reshape(bf16[256,256]{1,0:T(8,128)(2,1)} %param.9) | data formatting | bytes 262144 | tf_op jit(solution)/shard_map/reshape;squeeze;stack | solution.py:38
  10.1 1.7 %copy.33 = bf16[256,256]{0,1:T(8,128)(2,1)} copy(bf16[256,256]{1,0:T(8,128)(2,1)} %param.9) | data formatting | bytes 262144 | tf_op args[2]
  11.8 0.7 slice.25
  12.5 1.2 copy.27
  14.8 0.5 fusion.19
  15.7 1.9 %fusion.20 = f32[256,2,4,128]{3,0,2,1:T(8,128)} fusion(f32[2,256,256,4]{2,1,3,0:T(8,128)S(1)} %get-tuple-element.269, f32[2,4,256]{2,1,0:T(4,128)S(1)} %broadcast_maximum_fusion, pred[256,256]{0,1:T(8,128)(4,1)S(1)} %compare_and_fusion.1, f32[256,2,4]{0,2,1:T(4,128)S(1)} %get-tuple-element.266, bf16[256,2,128,1]{2,1,0,3:T(2,128)(2,1)S(1)} %bitcast.108), kind=kOutput, calls=%fused_computation.32 | convolution fusion | flops 137101312 | bytes 3358720 | tf_op jit(solution)/shard_map/avmk,kab->mavb/dot_general | solution.py:50
  17.6 87.5 %while.21 = (s32[]{:T(128)}, f32[2,4,256]{2,1,0:T(4,128)S(1)}, f32[2,4,256]{2,1,0:T(4,128)S(1)}, f32[256,2,4,128]{3,0,2,1:T(8,128)}, bf16[2,256,256]{1,2,0:T(8,1...) while((s32[]{:T(128)}, f32[2,4,256]{2,1,0:T(4,128)S(1)}, ...), condition=%wide.region_7.0_spmd.clone.clone, body=%wide.region_3.7_spmd.clone.clone.sunk | while | flops 276046848 | bytes 20062996 | solution.py:91
  17.6 4.9 %collective-permute-start = (bf16[2,256,256]{1,2,0:T(8,128)(2,1)S(1)}, bf16[2,256,256]{1,2,0:T(8,128)(2,1)S(1)}, u32[]{:S(2)}, u32[]{:S(2)}) collective-permute-start(bf16[2,256,256]{1,2,0:T(8,128)(2,1)S(1)} %get-tuple-element.356), channel_id=1, source_target_pairs={{0,4},{4,8},{8,12},{12,16},{16,20},{20,24},{24,28},{1,5},{5,9},{9,... | collective-permute-start | bytes 786440 | tf_op jit(solution)/shard_map/while/body/eval_jaxpr/ppermute | solution.py:16
  22.9 5.2 %collective-permute-done = bf16[2,256,256]{1,2,0:T(8,128)(2,1)S(1)} collective-permute-done((bf16[2,256,256]{1,2,0:T(8,128)(2,1)S(1)}, bf16[2,256,256]{1,2,0:T(8,128)(2,1)S(1)}, u32[]{:S(2)}, u32[]{:S(2)}) %collective-permute-start) | collective-permute-done | bytes 262176 | tf_op jit(solution)/shard_map/while/body/eval_jaxpr/ppermute | solution.py:16
  28.0 0.5 fusion.56
  29.3 1.1 fusion.59
  30.4 1.0 copy-done.1
  31.3 4.4 %collective-permute-start = (bf16[2,256,256]{1,2,0:T(8,128)(2,1)S(1)}, bf16[2,256,256]{1,2,0:T(8,128)(2,1)S(1)}, u32[]{:S(2)}, u32[]{:S(2)}) collective-permute-start(bf16[2,256,256]{1,2,0:T(8,128)(2,1)S(1)} %get-tuple-element.356), channel_id=1, source_target_pairs={{0,4},{4,8},{8,12},{12,16},{16,20},{20,24},{24,28},{1,5},{5,9},{9,... | collective-permute-start | bytes 786440 | tf_op jit(solution)/shard_map/while/body/eval_jaxpr/ppermute | solution.py:16
  36.1 4.3 %collective-permute-done = bf16[2,256,256]{1,2,0:T(8,128)(2,1)S(1)} collective-permute-done((bf16[2,256,256]{1,2,0:T(8,128)(2,1)S(1)}, bf16[2,256,256]{1,2,0:T(8,128)(2,1)S(1)}, u32[]{:S(2)}, u32[]{:S(2)}) %collective-permute-start) | collective-permute-done | bytes 262176 | tf_op jit(solution)/shard_map/while/body/eval_jaxpr/ppermute | solution.py:16
  40.4 0.5 fusion.56
  41.6 1.1 fusion.59
  42.7 1.0 copy-done.1
  43.7 4.4 %collective-permute-start = (bf16[2,256,256]{1,2,0:T(8,128)(2,1)S(1)}, bf16[2,256,256]{1,2,0:T(8,128)(2,1)S(1)}, u32[]{:S(2)}, u32[]{:S(2)}) collective-permute-start(bf16[2,256,256]{1,2,0:T(8,128)(2,1)S(1)} %get-tuple-element.356), channel_id=1, source_target_pairs={{0,4},{4,8},{8,12},{12,16},{16,20},{20,24},{24,28},{1,5},{5,9},{9,... | collective-permute-start | bytes 786440 | tf_op jit(solution)/shard_map/while/body/eval_jaxpr/ppermute | solution.py:16
  48.5 3.5 %collective-permute-done = bf16[2,256,256]{1,2,0:T(8,128)(2,1)S(1)} collective-permute-done((bf16[2,256,256]{1,2,0:T(8,128)(2,1)S(1)}, bf16[2,256,256]{1,2,0:T(8,128)(2,1)S(1)}, u32[]{:S(2)}, u32[]{:S(2)}) %collective-permute-start) | collective-permute-done | bytes 262176 | tf_op jit(solution)/shard_map/while/body/eval_jaxpr/ppermute | solution.py:16
  52.0 0.5 fusion.56
  53.2 1.1 fusion.59
  54.3 1.0 copy-done.1
  55.3 5.3 %collective-permute-start = (bf16[2,256,256]{1,2,0:T(8,128)(2,1)S(1)}, bf16[2,256,256]{1,2,0:T(8,128)(2,1)S(1)}, u32[]{:S(2)}, u32[]{:S(2)}) collective-permute-start(bf16[2,256,256]{1,2,0:T(8,128)(2,1)S(1)} %get-tuple-element.356), channel_id=1, source_target_pairs={{0,4},{4,8},{8,12},{12,16},{16,20},{20,24},{24,28},{1,5},{5,9},{9,... | collective-permute-start | bytes 786440 | tf_op jit(solution)/shard_map/while/body/eval_jaxpr/ppermute | solution.py:16
  60.9 3.5 %collective-permute-done = bf16[2,256,256]{1,2,0:T(8,128)(2,1)S(1)} collective-permute-done((bf16[2,256,256]{1,2,0:T(8,128)(2,1)S(1)}, bf16[2,256,256]{1,2,0:T(8,128)(2,1)S(1)}, u32[]{:S(2)}, u32[]{:S(2)}) %collective-permute-start) | collective-permute-done | bytes 262176 | tf_op jit(solution)/shard_map/while/body/eval_jaxpr/ppermute | solution.py:16
  64.4 0.5 fusion.56
  65.6 1.1 fusion.59
  66.8 1.0 copy-done.1
  67.7 5.3 %collective-permute-start = (bf16[2,256,256]{1,2,0:T(8,128)(2,1)S(1)}, bf16[2,256,256]{1,2,0:T(8,128)(2,1)S(1)}, u32[]{:S(2)}, u32[]{:S(2)}) collective-permute-start(bf16[2,256,256]{1,2,0:T(8,128)(2,1)S(1)} %get-tuple-element.356), channel_id=1, source_target_pairs={{0,4},{4,8},{8,12},{12,16},{16,20},{20,24},{24,28},{1,5},{5,9},{9,... | collective-permute-start | bytes 786440 | tf_op jit(solution)/shard_map/while/body/eval_jaxpr/ppermute | solution.py:16
  73.4 3.5 %collective-permute-done = bf16[2,256,256]{1,2,0:T(8,128)(2,1)S(1)} collective-permute-done((bf16[2,256,256]{1,2,0:T(8,128)(2,1)S(1)}, bf16[2,256,256]{1,2,0:T(8,128)(2,1)S(1)}, u32[]{:S(2)}, u32[]{:S(2)}) %collective-permute-start) | collective-permute-done | bytes 262176 | tf_op jit(solution)/shard_map/while/body/eval_jaxpr/ppermute | solution.py:16
  76.9 0.5 fusion.56
  78.1 1.1 fusion.59
  79.2 1.0 copy-done.1
  80.2 5.3 %collective-permute-start = (bf16[2,256,256]{1,2,0:T(8,128)(2,1)S(1)}, bf16[2,256,256]{1,2,0:T(8,128)(2,1)S(1)}, u32[]{:S(2)}, u32[]{:S(2)}) collective-permute-start(bf16[2,256,256]{1,2,0:T(8,128)(2,1)S(1)} %get-tuple-element.356), channel_id=1, source_target_pairs={{0,4},{4,8},{8,12},{12,16},{16,20},{20,24},{24,28},{1,5},{5,9},{9,... | collective-permute-start | bytes 786440 | tf_op jit(solution)/shard_map/while/body/eval_jaxpr/ppermute | solution.py:16
  85.8 3.5 %collective-permute-done = bf16[2,256,256]{1,2,0:T(8,128)(2,1)S(1)} collective-permute-done((bf16[2,256,256]{1,2,0:T(8,128)(2,1)S(1)}, bf16[2,256,256]{1,2,0:T(8,128)(2,1)S(1)}, u32[]{:S(2)}, u32[]{:S(2)}) %collective-permute-start) | collective-permute-done | bytes 262176 | tf_op jit(solution)/shard_map/while/body/eval_jaxpr/ppermute | solution.py:16
  89.4 0.5 fusion.56
  90.6 1.1 fusion.59
  91.7 1.0 copy-done.1
  92.6 5.3 %collective-permute-start = (bf16[2,256,256]{1,2,0:T(8,128)(2,1)S(1)}, bf16[2,256,256]{1,2,0:T(8,128)(2,1)S(1)}, u32[]{:S(2)}, u32[]{:S(2)}) collective-permute-start(bf16[2,256,256]{1,2,0:T(8,128)(2,1)S(1)} %get-tuple-element.356), channel_id=1, source_target_pairs={{0,4},{4,8},{8,12},{12,16},{16,20},{20,24},{24,28},{1,5},{5,9},{9,... | collective-permute-start | bytes 786440 | tf_op jit(solution)/shard_map/while/body/eval_jaxpr/ppermute | solution.py:16
  98.3 3.5 %collective-permute-done = bf16[2,256,256]{1,2,0:T(8,128)(2,1)S(1)} collective-permute-done((bf16[2,256,256]{1,2,0:T(8,128)(2,1)S(1)}, bf16[2,256,256]{1,2,0:T(8,128)(2,1)S(1)}, u32[]{:S(2)}, u32[]{:S(2)}) %collective-permute-start) | collective-permute-done | bytes 262176 | tf_op jit(solution)/shard_map/while/body/eval_jaxpr/ppermute | solution.py:16
  101.8 0.5 fusion.56
  103.0 1.1 fusion.59
  104.2 1.0 copy-done.1
  105.1 1.6 copy.35
  106.8 7.1 %fusion.16 = bf16[4096,256]{0,1:T(8,128)(2,1)} fusion(bf16[256,1024]{0,1:T(8,128)(2,1)S(1)} %bitcast.99, bf16[1024,4096]{1,0:T(8,128)(2,1)} %param.10), kind=kOutput, calls=%fused_computation.25 | convolution fusion | flops 2148532224 | bytes 11010048 | tf_op jit(solution)/shard_map/dot_general | solution.py:96
  113.9 35.6 %reduce-scatter.2.cloned.1.call-done = bf16[1024,256]{0,1:T(8,128)(2,1)} async-done(((bf16[4096,256]{0,1:T(8,128)(2,1)}), bf16[1024,256]{0,1:T(8,128)(2,1)}) %reduce-scatter.2.cloned.1.call-update) | async-done | bytes 524304 | tf_op jit(solution)/shard_map/reduce_scatter | solution.py:95
  149.6 2.0 %copy.36 = bf16[1024,256]{1,0:T(8,128)(2,1)} copy(bf16[1024,256]{0,1:T(8,128)(2,1)} %reduce-scatter.2.cloned.1.call-done) | data formatting | bytes 1048576 | tf_op jit(solution)/shard_map/reduce_scatter | solution.py:95
  (116 shorter events, 8.7 us)
Async XLA Ops:
  6.5 143.0 %reduce-scatter.2.cloned.1.call-start = ((), (), s32[]{:S(2)}) async-start(), calls=%async_computation.1 | async-start | bytes 2621440 | tf_op jit(solution)/shard_map/reduce_scatter | solution.py:95
  14.8 0.9 copy-start.3
  15.7 1.9 %copy-start.2 = (bf16[256,256]{0,1:T(8,128)(2,1)S(1)}, bf16[256,256]{0,1:T(8,128)(2,1)}, u32[]{:S(2)}) copy-start(bf16[256,256]{0,1:T(8,128)(2,1)} %copy.33) | copy-start | bytes 393220
  15.7 1.9 %copy-start.4 = (s32[5]{0:T(128)S(1)}, s32[5]{0:T(128)}, u32[]{:S(2)}) copy-start(s32[5]{0:T(128)} %param.11) | copy-start | bytes 64
  17.6 10.4 %collective-permute-start = (bf16[2,256,256]{1,2,0:T(8,128)(2,1)S(1)}, bf16[2,256,256]{1,2,0:T(8,128)(2,1)S(1)}, u32[]{:S(2)}, u32[]{:S(2)}) collective-permute-start(bf16[2,256,256]{1,2,0:T(8,128)(2,1)S(1)} %get-tuple-element.356), channel_id=1, source_target_pairs={{0,4},{4,8},{8,12},{12,16},{16,20},{20,24},{24,28},{1,5},{5,9},{9,... | collective-permute-start | bytes 786440 | tf_op jit(solution)/shard_map/while/body/eval_jaxpr/ppermute | solution.py:16
  28.0 1.2 copy-start
  30.3 1.0 copy-start.1
  31.3 9.1 %collective-permute-start = (bf16[2,256,256]{1,2,0:T(8,128)(2,1)S(1)}, bf16[2,256,256]{1,2,0:T(8,128)(2,1)S(1)}, u32[]{:S(2)}, u32[]{:S(2)}) collective-permute-start(bf16[2,256,256]{1,2,0:T(8,128)(2,1)S(1)} %get-tuple-element.356), channel_id=1, source_target_pairs={{0,4},{4,8},{8,12},{12,16},{16,20},{20,24},{24,28},{1,5},{5,9},{9,... | collective-permute-start | bytes 786440 | tf_op jit(solution)/shard_map/while/body/eval_jaxpr/ppermute | solution.py:16
  40.4 1.2 copy-start
  42.7 1.0 copy-start.1
  43.7 8.3 %collective-permute-start = (bf16[2,256,256]{1,2,0:T(8,128)(2,1)S(1)}, bf16[2,256,256]{1,2,0:T(8,128)(2,1)S(1)}, u32[]{:S(2)}, u32[]{:S(2)}) collective-permute-start(bf16[2,256,256]{1,2,0:T(8,128)(2,1)S(1)} %get-tuple-element.356), channel_id=1, source_target_pairs={{0,4},{4,8},{8,12},{12,16},{16,20},{20,24},{24,28},{1,5},{5,9},{9,... | collective-permute-start | bytes 786440 | tf_op jit(solution)/shard_map/while/body/eval_jaxpr/ppermute | solution.py:16
  52.0 1.2 copy-start
  54.3 1.0 copy-start.1
  55.3 9.1 %collective-permute-start = (bf16[2,256,256]{1,2,0:T(8,128)(2,1)S(1)}, bf16[2,256,256]{1,2,0:T(8,128)(2,1)S(1)}, u32[]{:S(2)}, u32[]{:S(2)}) collective-permute-start(bf16[2,256,256]{1,2,0:T(8,128)(2,1)S(1)} %get-tuple-element.356), channel_id=1, source_target_pairs={{0,4},{4,8},{8,12},{12,16},{16,20},{20,24},{24,28},{1,5},{5,9},{9,... | collective-permute-start | bytes 786440 | tf_op jit(solution)/shard_map/while/body/eval_jaxpr/ppermute | solution.py:16
  64.4 1.2 copy-start
  66.7 1.0 copy-start.1
  67.7 9.2 %collective-permute-start = (bf16[2,256,256]{1,2,0:T(8,128)(2,1)S(1)}, bf16[2,256,256]{1,2,0:T(8,128)(2,1)S(1)}, u32[]{:S(2)}, u32[]{:S(2)}) collective-permute-start(bf16[2,256,256]{1,2,0:T(8,128)(2,1)S(1)} %get-tuple-element.356), channel_id=1, source_target_pairs={{0,4},{4,8},{8,12},{12,16},{16,20},{20,24},{24,28},{1,5},{5,9},{9,... | collective-permute-start | bytes 786440 | tf_op jit(solution)/shard_map/while/body/eval_jaxpr/ppermute | solution.py:16
  76.9 1.2 copy-start
  79.2 1.0 copy-start.1
  80.2 9.2 %collective-permute-start = (bf16[2,256,256]{1,2,0:T(8,128)(2,1)S(1)}, bf16[2,256,256]{1,2,0:T(8,128)(2,1)S(1)}, u32[]{:S(2)}, u32[]{:S(2)}) collective-permute-start(bf16[2,256,256]{1,2,0:T(8,128)(2,1)S(1)} %get-tuple-element.356), channel_id=1, source_target_pairs={{0,4},{4,8},{8,12},{12,16},{16,20},{20,24},{24,28},{1,5},{5,9},{9,... | collective-permute-start | bytes 786440 | tf_op jit(solution)/shard_map/while/body/eval_jaxpr/ppermute | solution.py:16
  89.4 1.2 copy-start
  91.7 1.0 copy-start.1
  92.6 9.2 %collective-permute-start = (bf16[2,256,256]{1,2,0:T(8,128)(2,1)S(1)}, bf16[2,256,256]{1,2,0:T(8,128)(2,1)S(1)}, u32[]{:S(2)}, u32[]{:S(2)}) collective-permute-start(bf16[2,256,256]{1,2,0:T(8,128)(2,1)S(1)} %get-tuple-element.356), channel_id=1, source_target_pairs={{0,4},{4,8},{8,12},{12,16},{16,20},{20,24},{24,28},{1,5},{5,9},{9,... | collective-permute-start | bytes 786440 | tf_op jit(solution)/shard_map/while/body/eval_jaxpr/ppermute | solution.py:16
  101.8 1.2 copy-start
  104.1 1.0 copy-start.1
Sparse Core Ops, SparseCore 0:
  114.0 35.4 reduce-scatter.1
where the time goes:
time: 159 us; the launch traced here: 158 us
  waiting for transfers between devices  62.6 us (39%)
  starting transfers between devices  34.8 us (22%)
  matrix products  20.8 us (13%)
  local copies, waits for them, and re-layouts  19.5 us (12%)
  between operations  13.5 us (8%)
  other arithmetic  6.65 us (4%)
    reduce_scatter x1, waiting for transfers between devices, on_device(): lax.psum_scatter(lax.dot_general(out_weight, attended, (((0,), (1,)), (()...  35.6 us
    ppermute x7, starting transfers between devices, shifted(): return lax.ppermute(block, axis, route)  34.8 us
    ppermute x7, waiting for transfers between devices, shifted(): return lax.ppermute(block, axis, route)  26.9 us
    dot_general x8, matrix products, attend(): jnp.einsum('avmk,kab->mavb', attention_probs.astype(jnp.bfloat16), value_...  9.39 us
    while x42, local copies, waits for them, and re-layouts  7.51 us
    dot_general x1, matrix products, on_device(): lax.dot_general(out_weight, attended, (((0,), (1,)), ((), ())), preferred...  7.11 us
    unnamed x10, local copies, waits for them, and re-layouts  4.52 us
    dot_general x8, matrix products, attend(): jnp.einsum('myqe,cye->yqmc', query_head_rows, grouped_key_heads, preferre...  4.31 us
  transfers between devices with their start and end apart: 8, of which 8 were waited for; matrix products, arithmetic and copies ran while one was open for 2% of the time, Pallas kernels for 0%

commit v1 on v0

v1 whole, which is shorter than its diff:
```python
import jax
import jax.numpy as jnp
from jax import lax
from jax.experimental import pallas as pl
from jax.experimental.pallas import tpu as pltpu
from jax.sharding import PartitionSpec as P

HEAD_DIM = 128
REACH = 15
LOG2E = 1.4426950408889634
masked_score = -1e30
VMEM_LIMIT = 48 * 1024 * 1024

vmem = pl.BlockSpec(memory_space=pltpu.VMEM)
smem = pl.BlockSpec(memory_space=pltpu.SMEM)
anywhere = pl.BlockSpec(memory_space=pl.ANY)


def params():
    return pltpu.CompilerParams(vmem_limit_bytes=VMEM_LIMIT)


def document_starts(where, rows):
    first = where[0] * rows
    positions = first + lax.broadcasted_iota(jnp.int32, (1, rows), 1)
    starts = jnp.zeros((1, rows), jnp.int32)
    start_first = jnp.int32(0)
    start_last = jnp.int32(0)
    for i in range(2, where.shape[0] - 1):
        edge = where[i]
        starts = jnp.where(positions >= edge, edge, starts)
        start_first = jnp.where(first >= edge, edge, start_first)
        start_last = jnp.where(first + rows - 1 >= edge, edge, start_last)
    return positions, starts, start_first, start_last


def scores_of(keys, query):
    return lax.dot_general(keys, query, (((1,), (1,)), ((), ())), preferred_element_type=jnp.float32)


def attend_piece(q_ref, kv_ref, group, heads, before, after, key_start, positions, starts):
    rows = kv_ref.shape[0]
    factor = HEAD_DIM ** -0.5 * LOG2E
    keys = kv_ref[:, :HEAD_DIM]
    values = kv_ref[:, HEAD_DIM:].T
    key_pos = key_start + lax.broadcasted_iota(jnp.int32, (rows, 1), 0)
    visible = key_pos >= starts
    if before is None:
        visible = visible & (key_pos <= positions)
    for i in range(heads):
        h = group * heads + i
        s = scores_of(keys, q_ref[:, h * HEAD_DIM : (h + 1) * HEAD_DIM])
        s = jnp.where(visible, s, masked_score)
        top = jnp.max(s, axis=0, keepdims=True)
        if before is not None:
            old_top = before[0][i : i + 1, :]
            top = jnp.maximum(old_top, top)
        p = jnp.exp2((s - top) * factor)
        total = jnp.sum(p, axis=0, keepdims=True)
        out = jnp.dot(values, p.astype(jnp.bfloat16), preferred_element_type=jnp.float32)
        if before is not None:
            alpha = jnp.exp2((old_top - top) * factor)
            total = before[1][i : i + 1, :] * alpha + total
            out = before[2][i] * alpha + out
        after[0][i : i + 1, :] = top
        after[1][i : i + 1, :] = total
        after[2][i] = out


def attend_pieces(where, q_ref, pieces, before, after, heads):
    rows = q_ref.shape[0]
    me = where[0]
    positions, starts, start_first, _ = document_starts(where, rows)
    current = dict(before)
    for kv_ref, group, back, own in pieces:
        key_start = (me - back(lax.rem(me, 2))) * rows
        if own:
            attend_piece(q_ref, kv_ref, group, heads, None, after[group], key_start, positions, starts)
        else:
            seen = (key_start >= 0) & (key_start + rows > start_first)
            source = current[group]

            @pl.when(seen)
            def _():
                attend_piece(q_ref, kv_ref, group, heads, source, after[group], key_start, positions, starts)

            if source is not after[group]:

                @pl.when(jnp.logical_not(seen))
                def _():
                    for old, new in zip(source, after[group]):
                        new[...] = old[...]

        current[group] = after[group]


def state_shapes(heads, rows):
    return [(heads, rows), (heads, rows), (heads, HEAD_DIM, rows)]


def by_threes(refs, groups):
    return {g: refs[3 * i : 3 * i + 3] for i, g in enumerate(groups)}


def attend_call(where, q, pieces, state, n_groups):
    rows, width = q.shape
    heads = width // HEAD_DIM // n_groups
    touched = sorted({p[1] for p in pieces})
    given = [a for g in touched for a in state.get(g, ())]

    def kernel(where_ref, q_ref, *refs):
        kvs = refs[: len(pieces)]
        before = by_threes(refs[len(pieces) : len(pieces) + len(given)], touched) if given else {}
        after = by_threes(refs[len(pieces) + len(given) :], touched)
        attend_pieces(where_ref, q_ref, [(r, *p[1:]) for r, p in zip(kvs, pieces)], before, after, heads)

    shapes = [jax.ShapeDtypeStruct(s, jnp.float32) for s in state_shapes(heads, rows) * len(touched)]
    first = 2 + len(pieces)
    outs = pl.pallas_call(
        kernel,
        out_shape=shapes,
        in_specs=[smem] + [vmem] * (1 + len(pieces) + len(given)),
        out_specs=[vmem] * len(shapes),
        input_output_aliases={first + i: i for i in range(len(given))},
        compiler_params=params(),
        name="attend",
    )(where, q, *[p[0] for p in pieces], *given)
    return {**state, **by_threes(outs, touched)}


def finish_call(where, q, pieces, state, n_groups):
    rows, width = q.shape
    n_heads = width // HEAD_DIM
    heads = n_heads // n_groups
    groups = range(n_groups)
    given = [a for g in groups for a in state[g]]

    def kernel(where_ref, q_ref, *refs):
        kvs = refs[: len(pieces)]
        before = by_threes(refs[len(pieces) : len(pieces) + len(given)], groups)
        out_ref = refs[len(pieces) + len(given)]
        after = by_threes(refs[len(pieces) + len(given) + 1 :], groups)
        attend_pieces(where_ref, q_ref, [(r, *p[1:]) for r, p in zip(kvs, pieces)], before, after, heads)
        for h in range(n_heads):
            _, total_ref, acc_ref = after[h // heads]
            i = h % heads
            head = acc_ref[i] / total_ref[i : i + 1, :]
            out_ref[:, h * HEAD_DIM : (h + 1) * HEAD_DIM] = head.T.astype(jnp.bfloat16)

    return pl.pallas_call(
        kernel,
        out_shape=jax.ShapeDtypeStruct((rows, width), jnp.bfloat16),
        in_specs=[smem] + [vmem] * (1 + len(pieces) + len(given)),
        out_specs=vmem,
        scratch_shapes=[pltpu.VMEM(s, jnp.float32) for s in state_shapes(heads, rows) * n_groups],
        compiler_params=params(),
        name="finish",
    )(where, q, *[p[0] for p in pieces], *given)


def project_call(attended, out_weight, blocks, block, added, out_type, name):
    rows, depth = attended.shape
    count = len(blocks)

    def kernel(order_ref, att_ref, w_ref, *refs):
        out_ref, w_scratch, sems = refs[-3:]
        copies = []
        for i in range(count):
            start = pl.multiple_of(order_ref[i] * block, block)
            copy = pltpu.make_async_copy(w_ref.at[:, pl.ds(start, block)], w_scratch.at[i], sems.at[i])
            copy.start()
            copies.append(copy)
        for i in range(count):
            copies[i].wait()
            value = jnp.dot(att_ref[...], w_scratch[i], preferred_element_type=jnp.float32)
            if added is not None:
                value = value + refs[0][i].astype(jnp.float32)
            out_ref[i] = value.astype(out_type)

    more = [] if added is None else [added]
    return pl.pallas_call(
        kernel,
        out_shape=jax.ShapeDtypeStruct((count, rows, block), out_type),
        in_specs=[smem, vmem, anywhere] + [vmem] * len(more),
        out_specs=vmem,
        scratch_shapes=[pltpu.VMEM((count, depth, block), jnp.bfloat16), pltpu.SemaphoreType.DMA((count,))],
        compiler_params=params(),
        name=name,
    )(jnp.stack(blocks).astype(jnp.int32), attended, out_weight, *more)


def output_call(kept, arrived):
    rows, block = kept.shape

    def kernel(kept_ref, arrived_ref, out_ref):
        out_ref[...] = (kept_ref[...] + arrived_ref[...].astype(jnp.float32)).T.astype(jnp.bfloat16)

    return pl.pallas_call(
        kernel,
        out_shape=jax.ShapeDtypeStruct((block, rows), jnp.bfloat16),
        in_specs=[vmem] * 2,
        out_specs=vmem,
        compiler_params=params(),
        name="output",
    )(kept, arrived)


def swapped(array, axis, bit):
    return lax.ppermute(array, axis, [(i, i ^ bit) for i in range(lax.axis_size(axis))])


def projected(attended, out_weight):
    count = lax.axis_size("head")
    block = out_weight.shape[1] // count
    me = lax.axis_index("head")
    if count < 4 or count & (count - 1):
        whole = jnp.dot(attended, out_weight, preferred_element_type=jnp.float32).astype(jnp.bfloat16)
        return lax.psum_scatter(whole, "head", scatter_dimension=1, tiled=True).T
    mine = [(me >> b) & 1 for b in range(count.bit_length() - 1)]

    def blocks(bit0, bit1):
        return [bit0 + 2 * bit1 + 4 * i for i in range(count // 4)]

    send_far = project_call(attended, out_weight, blocks(1 - mine[0], 1 - mine[1]), block, None, jnp.bfloat16, "p0")
    got_far = swapped(send_far, "head", 1)
    send_near = project_call(attended, out_weight, blocks(1 - mine[0], mine[1]), block, None, jnp.bfloat16, "p1")
    got_near = swapped(send_near, "head", 1)
    far = project_call(attended, out_weight, blocks(mine[0], 1 - mine[1]), block, got_far, jnp.bfloat16, "p2")
    got = swapped(far, "head", 2)
    kept = project_call(attended, out_weight, blocks(mine[0], mine[1]), block, got_near, jnp.float32, "p3")
    for b in range(2, len(mine)):
        kept = kept + got.astype(jnp.float32)
        pairs = kept.reshape(kept.shape[0] // 2, 2, *kept.shape[1:])
        sent = lax.dynamic_index_in_dim(pairs, 1 - mine[b], 1, keepdims=False)
        kept = lax.dynamic_index_in_dim(pairs, mine[b], 1, keepdims=False)
        got = swapped(sent.astype(jnp.bfloat16), "head", 1 << b)
    return output_call(kept[0], got[0])


def on_device(queries, key_vectors, value_vectors, out_weight, offsets):
    rows = queries.shape[0]
    groups = key_vectors.shape[1] // HEAD_DIM
    devices = lax.axis_size("ctx")
    me = lax.axis_index("ctx")
    odd = lax.rem(me, 2) == 1
    pair_steps = (min(REACH, devices // 2) + 1) // 2
    where = jnp.concatenate([me[None].astype(jnp.int32), offsets])

    def shifted(block):
        return lax.ppermute(block, "ctx", [(i, (i + 2) % devices) for i in range(devices)])

    def piece(g):
        cut = slice(g * HEAD_DIM, (g + 1) * HEAD_DIM)
        return jnp.concatenate([key_vectors[:, cut], value_vectors[:, cut]], axis=1)

    own = [piece(g) for g in range(groups)]
    moving = own
    state = attend_call(where, queries, [(own[g], g, lambda x: 0, True) for g in range(groups)], {}, groups)
    for step in range(1, pair_steps + 1):
        moving = [shifted(m) for m in moving]
        last = step == pair_steps
        across = [swapped(jnp.where(odd, m, o) if last else m, "ctx", 1) for m, o in zip(moving, own)]
        back = (lambda x, step=step: jnp.where(x == 1, 1, 2 * step - 1)) if last else (lambda x, step=step: 2 * step - 1 + 2 * x)
        pieces = [(moving[g], g, lambda x, step=step: 2 * step, False) for g in range(groups)]
        state = attend_call(where, queries, pieces, state, groups)
        pieces = [(across[g], g, back, False) for g in range(groups)]
        if last:
            attended = finish_call(where, queries, pieces, state, groups)
        else:
            state = attend_call(where, queries, pieces, state, groups)
    return projected(attended, out_weight)


def solution(mesh):
    placed = (P("ctx", "head"), P("ctx", "head"), P("ctx", "head"), P("head", None), P())
    return jax.shard_map(
        on_device, mesh=mesh, in_specs=placed, out_specs=P("head", "ctx"), check_vma=False
    )
```

time: 159 us -> 59.2 us (0.37)
  the two profiles are of different devices: /device:TPU:0 before, /device:TPU:24 now
where the time goes in v1:
time: 59.2 us; the launch traced here: 58.9 us
  Pallas kernels  25.7 us (43%)
  waiting for transfers between devices  16.3 us (28%)
  starting transfers between devices  12.8 us (22%)
  local copies, waits for them, and re-layouts  3.03 us (5%)
  other arithmetic  0.83 us (1%)
    pallas_call x4, Pallas kernels, attend_call(): pl.pallas_call(kernel, out_shape=shapes, in_specs=[smem] + [vmem] * (1 +...  12 us
    ppermute x7, waiting for transfers between devices, swapped(): lax.ppermute(array, axis, [(i, i ^ bit) for i in range(lax.axis_size(axis...  10 us
    pallas_call x4, Pallas kernels, project_call(): pl.pallas_call(kernel, out_shape=jax.ShapeDtypeStruct((count, rows, block...  9.25 us
    ppermute x7, starting transfers between devices, swapped(): lax.ppermute(array, axis, [(i, i ^ bit) for i in range(lax.axis_size(axis...  8.23 us
    ppermute x4, waiting for transfers between devices, shifted(): lax.ppermute(block, 'ctx', [(i, (i + 2) % devices) for i in range(devices)])  6.3 us
    ppermute x4, starting transfers between devices, shifted(): lax.ppermute(block, 'ctx', [(i, (i + 2) % devices) for i in range(devices)])  4.59 us
    pallas_call x1, Pallas kernels, finish_call(): pl.pallas_call(kernel, out_shape=jax.ShapeDtypeStruct((rows, width), jnp....  3.37 us
    unnamed x4, local copies, waits for them, and re-layouts  2.08 us
  transfers between devices with their start and end apart: 11, of which 4 were waited for; matrix products, arithmetic and copies ran while one was open for 1% of the time, Pallas kernels for 32%

profile of v1, /device:TPU:24, one launch (start us, length us, event | category | flops | bytes accessed | tf_op | source)
XLA Modules:
  0.0 58.9 jit_solution(847540317476747847)
XLA Ops:
  0.0 1.0 %fusion = (bf16[256,128]{1,0:T(8,128)(2,1)S(1)}, bf16[256,128]{1,0:T(8,128)(2,1)S(1)}, bf16[256,128]{1,0:T(8,128)(2,1)S(1)}, bf16[256,128]{1,0:T(8,128)(2,1)S(1)}) fusion(bf16[256,256]{1,0:T(8,128)(2,1)} %param.6, bf16[256,256]{1,0:T(8,128)(2,1)} %param.7), kind=kLoop, calls=%fused_computation.5 | loop fusion | bytes 524288 | tf_op jit(solution)/shard_map/slice | solution.py:254
  1.0 0.1 collective-permute-start.3
  1.1 1.8 %collective-permute-start = (bf16[256,256]{1,0:T(8,128)(2,1)S(1)}, bf16[256,256]{1,0:T(8,128)(2,1)S(1)}, u32[]{:S(2)}, u32[]{:S(2)}) collective-permute-start(bf16[256,256]{1,0:T(8,128)(2,1)S(1)} %pad_maximum_fusion.refs_0_), channel_id=1, source_target_pairs={{0,8},{4,12},{8,16},{12,20},{16,24},{20,28},{24,0},{28,4},{1,9},{5... | collective-permute-start | bytes 393224 | tf_op jit(solution)/shard_map/ppermute | solution.py:250
  2.9 4.5 %collective-permute-done.3.refs_1_ = bf16[256,256]{1,0:T(8,128)(2,1)S(1)} collective-permute-done((bf16[256,256]{1,0:T(8,128)(2,1)S(1)}, bf16[256,256]{1,0:T(8,128)(2,1)S(1)}, u32[]{:S(2)}, u32[]{:S(2)}) %collective-permute-start.3) | collective-permute-done | bytes 131104 | tf_op jit(solution)/shard_map/ppermute | solution.py:250
  7.4 1.8 %collective-permute-start.4 = (bf16[256,256]{1,0:T(8,128)(2,1)S(1)}, bf16[256,256]{1,0:T(8,128)(2,1)S(1)}, u32[]{:S(2)}, u32[]{:S(2)}) collective-permute-start(bf16[256,256]{1,0:T(8,128)(2,1)S(1)} %collective-permute-done.3.refs_1_), channel_id=1, source_target_pairs={{0,8},{4,12},{8,16},{12,20},{16,24},{20,28},{24,0},{28,4},{1,9},{5... | collective-permute-start | bytes 393224 | tf_op jit(solution)/shard_map/ppermute | solution.py:250
  9.2 1.7 %collective-permute-start.7 = (bf16[256,256]{1,0:T(8,128)(2,1)S(1)}, bf16[256,256]{1,0:T(8,128)(2,1)S(1)}, u32[]{:S(2)}, u32[]{:S(2)}) collective-permute-start(bf16[256,256]{1,0:T(8,128)(2,1)S(1)} %collective-permute-done.3.refs_1_), channel_id=1, source_target_pairs={{0,4},{4,0},{8,12},{12,8},{16,20},{20,16},{24,28},{28,24},{1,5},{5... | collective-permute-start | bytes 393224 | tf_op jit(solution)/shard_map/ppermute | solution.py:209
  10.9 0.0 collective-permute-done.refs_0_
  10.9 0.8 %collective-permute-start.6 = (bf16[256,256]{1,0:T(8,128)(2,1)S(1)}, bf16[256,256]{1,0:T(8,128)(2,1)S(1)}, u32[]{:S(2)}, u32[]{:S(2)}) collective-permute-start(bf16[256,256]{1,0:T(8,128)(2,1)S(1)} %collective-permute-done.refs_0_), channel_id=1, source_target_pairs={{0,4},{4,0},{8,12},{12,8},{16,20},{20,16},{24,28},{28,24},{1,5},{5... | collective-permute-start | bytes 393224 | tf_op jit(solution)/shard_map/ppermute | solution.py:209
  11.7 0.9 %collective-permute-start.1 = (bf16[256,256]{1,0:T(8,128)(2,1)S(1)}, bf16[256,256]{1,0:T(8,128)(2,1)S(1)}, u32[]{:S(2)}, u32[]{:S(2)}) collective-permute-start(bf16[256,256]{1,0:T(8,128)(2,1)S(1)} %collective-permute-done.refs_0_), channel_id=1, source_target_pairs={{0,8},{4,12},{8,16},{12,20},{16,24},{20,28},{24,0},{28,4},{1,9},{5... | collective-permute-start | bytes 393224 | tf_op jit(solution)/shard_map/ppermute | solution.py:250
  12.7 0.3 collective-permute-done.4.refs_1_
  13.0 2.2 %collective-permute-start.5 = (bf16[256,256]{1,0:T(8,128)(2,1)S(1)}, bf16[256,256]{1,0:T(8,128)(2,1)S(1)}, u32[]{:S(2)}, u32[]{:S(2)}) collective-permute-start(bf16[256,256]{1,0:T(8,128)(2,1)S(1)} %broadcast_select_fusion), channel_id=1, source_target_pairs={{0,4},{4,0},{8,12},{12,8},{16,20},{20,16},{24,28},{28,24},{1,5},{5... | collective-permute-start | bytes 393224 | tf_op jit(solution)/shard_map/ppermute | solution.py:209
  15.2 1.5 %collective-permute-done.1.refs_0_ = bf16[256,256]{1,0:T(8,128)(2,1)S(1)} collective-permute-done((bf16[256,256]{1,0:T(8,128)(2,1)S(1)}, bf16[256,256]{1,0:T(8,128)(2,1)S(1)}, u32[]{:S(2)}, u32[]{:S(2)}) %collective-permute-start.1) | collective-permute-done | bytes 131104 | tf_op jit(solution)/shard_map/ppermute | solution.py:250
  16.7 1.3 %collective-permute-start.2 = (bf16[256,256]{1,0:T(8,128)(2,1)S(1)}, bf16[256,256]{1,0:T(8,128)(2,1)S(1)}, u32[]{:S(2)}, u32[]{:S(2)}) collective-permute-start(bf16[256,256]{1,0:T(8,128)(2,1)S(1)} %broadcast_select_fusion.1), channel_id=1, source_target_pairs={{0,4},{4,0},{8,12},{12,8},{16,20},{20,16},{24,28},{28,24},{1,5},{5... | collective-permute-start | bytes 393224 | tf_op jit(solution)/shard_map/ppermute | solution.py:209
  18.0 0.7 %pad_add_fusion.where_ref = s32[6]{0:T(128)S(1)} fusion(s32[5]{0:T(128)} %param.9, s32[1]{0:T(128)} %bitcast.1), kind=kLoop, calls=%fused_computation.4 | loop fusion | flops 6 | bytes 48 | tf_op jit(solution)/shard_map/concatenate | solution.py:247
  18.8 0.0 copy-start
  18.8 1.0 %copy-done = bf16[256,1024]{1,0:T(8,128)(2,1)S(1)} copy-done((bf16[256,1024]{1,0:T(8,128)(2,1)S(1)}, bf16[256,1024]{1,0:T(8,128)(2,1)}, u32[]{:S(2)}) %copy-start) | copy-done | bytes 524312
  19.8 3.0 %attend.4 = (f32[4,256]{1,0:T(4,128)S(1)}, f32[4,256]{1,0:T(4,128)S(1)}, f32[4,128,256]{2,1,0:T(8,128)S(1)}, f32[4,256]{1,0:T(4,128)S(1)}, f32[4,256]{1,0:T(4,128)S(1)}, /*index=5*/f32[4,128,256]{2,1,0:T(8,128)S(1)}) custom-call(s32[6]{0:T(128)S(1)} %pad_add_fusion.where_ref, bf16[256,1024]{1,0:T(8,128)(2,1)S(1)} %copy-done, ...), custom_call_target="tpu_custom_call" | custom-call | tf_op jit(solution)/shard_map/attend/pallas_call | solution.py:119
  22.8 0.0 copy-start.1
  22.8 1.0 %copy-done.1 = bf16[256,1024]{1,0:T(8,128)(2,1)S(1)} copy-done((bf16[256,1024]{1,0:T(8,128)(2,1)S(1)}, bf16[256,1024]{1,0:T(8,128)(2,1)}, u32[]{:S(2)}) %copy-start.1) | copy-done | bytes 524312
  23.9 3.0 %attend.5 = (f32[4,256]{1,0:T(4,128)S(1)}, f32[4,256]{1,0:T(4,128)S(1)}, f32[4,128,256]{2,1,0:T(8,128)S(1)}, f32[4,256]{1,0:T(4,128)S(1)}, f32[4,256]{1,0:T(4,128)S(1)}, /*index=5*/f32[4,128,256]{2,1,0:T(8,128)S(1)}) custom-call(s32[6]{0:T(128)S(1)} %pad_add_fusion.where_ref, ...), custom_call_target="tpu_custom_call", output_to_operand_aliasing={{0}: (4, {}), {1}: (5, {}), {2}: (6, {}), {3}: (7, {}), {4}... | custom-call | tf_op jit(solution)/shard_map/attend/pallas_call | solution.py:119
  26.9 0.0 collective-permute-done.7.refs_1_
  26.9 0.0 collective-permute-done.6.refs_0_
  26.9 3.0 %attend.6 = (f32[4,256]{1,0:T(4,128)S(1)}, f32[4,256]{1,0:T(4,128)S(1)}, f32[4,128,256]{2,1,0:T(8,128)S(1)}, f32[4,256]{1,0:T(4,128)S(1)}, f32[4,256]{1,0:T(4,128)S(1)}, /*index=5*/f32[4,128,256]{2,1,0:T(8,128)S(1)}) custom-call(s32[6]{0:T(128)S(1)} %pad_add_fusion.where_ref, ...), custom_call_target="tpu_custom_call", output_to_operand_aliasing={{0}: (4, {}), {1}: (5, {}), {2}: (6, {}), {3}: (7, {}), {4}... | custom-call | tf_op jit(solution)/shard_map/attend/pallas_call | solution.py:119
  29.9 3.0 %attend.7 = (f32[4,256]{1,0:T(4,128)S(1)}, f32[4,256]{1,0:T(4,128)S(1)}, f32[4,128,256]{2,1,0:T(8,128)S(1)}, f32[4,256]{1,0:T(4,128)S(1)}, f32[4,256]{1,0:T(4,128)S(1)}, /*index=5*/f32[4,128,256]{2,1,0:T(8,128)S(1)}) custom-call(s32[6]{0:T(128)S(1)} %pad_add_fusion.where_ref, ...), custom_call_target="tpu_custom_call", output_to_operand_aliasing={{0}: (4, {}), {1}: (5, {}), {2}: (6, {}), {3}: (7, {}), {4}... | custom-call | tf_op jit(solution)/shard_map/attend/pallas_call | solution.py:119
  32.9 0.0 collective-permute-done.5.refs_1_
  32.9 0.0 collective-permute-done.2.refs_0_
  33.0 3.4 %finish.1.att_ref = bf16[256,1024]{1,0:T(8,128)(2,1)S(1)} custom-call(s32[6]{0:T(128)S(1)} %pad_add_fusion.where_ref, bf16[256,1024]{1,0:T(8,128)(2,1)S(1)} %copy-done.1, bf16[256,256]{1,0:T(8,128)(2,1)S(1)} %collective-permute-done.2.refs_0_, bf16[256,256]{1,0:T(8,128)(2,1)S(1)} %collective-permute-done.5.refs_1_, f32[4,256]{1,0:T(4,128)S(1)} %get-tuple-element.47.refs_2_, ...), custom_call_target="tpu_custom_call" | custom-call | tf_op jit(solution)/shard_map/finish/pallas_call | solution.py:150
  36.3 2.3 %p0.1 = bf16[1,256,1024]{2,1,0:T(8,128)(2,1)S(1)} custom-call(s32[1]{0:T(128)} %bitcast.5.order_ref, bf16[256,1024]{1,0:T(8,128)(2,1)S(1)} %finish.1.att_ref, bf16[1024,4096]{1,0:T(8,128)(2,1)} %w_ref.7), custom_call_target="tpu_custom_call" | custom-call | tf_op jit(solution)/shard_map/p0/pallas_call | solution.py:181
  38.6 0.1 collective-permute-start.9
  38.7 2.3 %p1.1 = bf16[1,256,1024]{2,1,0:T(8,128)(2,1)S(1)} custom-call(s32[1]{0:T(128)} %bitcast.2.order_ref, bf16[256,1024]{1,0:T(8,128)(2,1)S(1)} %finish.1.att_ref, bf16[1024,4096]{1,0:T(8,128)(2,1)} %w_ref.7), custom_call_target="tpu_custom_call" | custom-call | tf_op jit(solution)/shard_map/p1/pallas_call | solution.py:181
  41.1 0.5 collective-permute-start.8
  41.6 0.0 collective-permute-done.9.refs_0_
  41.6 2.3 %p2.1 = bf16[1,256,1024]{2,1,0:T(8,128)(2,1)S(1)} custom-call(s32[1]{0:T(128)} %bitcast.4.order_ref, bf16[256,1024]{1,0:T(8,128)(2,1)S(1)} %finish.1.att_ref, bf16[1024,4096]{1,0:T(8,128)(2,1)} %w_ref.7, bf16[1,256,1024]{2,1,0:T(8,128)(2,1)S(1)} %collective-permute-done.9.refs_0_), custom_call_target="tpu_custom_call" | custom-call | tf_op jit(solution)/shard_map/p2/pallas_call | solution.py:181
  43.9 1.6 %collective-permute-start.10 = (bf16[1,256,1024]{2,1,0:T(8,128)(2,1)S(1)}, bf16[1,256,1024]{2,1,0:T(8,128)(2,1)S(1)}, u32[]{:S(2)}, u32[]{:S(2)}) collective-permute-start(bf16[1,256,1024]{2,1,0:T(8,128)(2,1)S(1)} %p2.1), channel_id=1, source_target_pairs={{0,2},{1,3},{2,0},{3,1},{4,6},{5,7},{6,4},{7,5},{8,10},{9,11},{10,... | collective-permute-start | bytes 1572872 | tf_op jit(solution)/shard_map/ppermute | solution.py:209
  45.5 0.0 collective-permute-done.8.refs_0_
  45.5 2.3 %p3.1 = f32[1,256,1024]{2,1,0:T(8,128)S(1)} custom-call(s32[1]{0:T(128)} %bitcast.order_ref, bf16[256,1024]{1,0:T(8,128)(2,1)S(1)} %finish.1.att_ref, bf16[1024,4096]{1,0:T(8,128)(2,1)} %w_ref.7, bf16[1,256,1024]{2,1,0:T(8,128)(2,1)S(1)} %collective-permute-done.8.refs_0_), custom_call_target="tpu_custom_call" | custom-call | tf_op jit(solution)/shard_map/p3/pallas_call | solution.py:181
  47.8 10.0 %collective-permute-done.10 = bf16[1,256,1024]{2,1,0:T(8,128)(2,1)S(1)} collective-permute-done((bf16[1,256,1024]{2,1,0:T(8,128)(2,1)S(1)}, bf16[1,256,1024]{2,1,0:T(8,128)(2,1)S(1)}, u32[]{:S(2)}, u32[]{:S(2)}) %collective-permute-start.10) | collective-permute-done | bytes 524320 | tf_op jit(solution)/shard_map/ppermute | solution.py:209
  57.9 1.0 %output.1 = bf16[1024,256]{1,0:T(8,128)(2,1)} custom-call(f32[256,1024]{1,0:T(8,128)S(1)} %bitcast.7, bf16[256,1024]{1,0:T(8,128)(2,1)S(1)} %bitcast.8), custom_call_target="tpu_custom_call" | custom-call | tf_op jit(solution)/shard_map/output/pallas_call | solution.py:198
  (4 shorter events, 0.1 us)
Async XLA Ops:
  1.0 6.4 %collective-permute-start.3 = (bf16[256,256]{1,0:T(8,128)(2,1)S(1)}, bf16[256,256]{1,0:T(8,128)(2,1)S(1)}, u32[]{:S(2)}, u32[]{:S(2)}) collective-permute-start(bf16[256,256]{1,0:T(8,128)(2,1)S(1)} %pad_maximum_fusion.1.refs_1_), channel_id=1, source_target_pairs={{0,8},{4,12},{8,16},{12,20},{16,24},{20,28},{24,0},{28,4},{1,9},{5... | collective-permute-start | bytes 393224 | tf_op jit(solution)/shard_map/ppermute | solution.py:250
  1.1 9.9 %collective-permute-start = (bf16[256,256]{1,0:T(8,128)(2,1)S(1)}, bf16[256,256]{1,0:T(8,128)(2,1)S(1)}, u32[]{:S(2)}, u32[]{:S(2)}) collective-permute-start(bf16[256,256]{1,0:T(8,128)(2,1)S(1)} %pad_maximum_fusion.refs_0_), channel_id=1, source_target_pairs={{0,8},{4,12},{8,16},{12,20},{16,24},{20,28},{24,0},{28,4},{1,9},{5... | collective-permute-start | bytes 393224 | tf_op jit(solution)/shard_map/ppermute | solution.py:250
  7.4 5.5 %collective-permute-start.4 = (bf16[256,256]{1,0:T(8,128)(2,1)S(1)}, bf16[256,256]{1,0:T(8,128)(2,1)S(1)}, u32[]{:S(2)}, u32[]{:S(2)}) collective-permute-start(bf16[256,256]{1,0:T(8,128)(2,1)S(1)} %collective-permute-done.3.refs_1_), channel_id=1, source_target_pairs={{0,8},{4,12},{8,16},{12,20},{16,24},{20,28},{24,0},{28,4},{1,9},{5... | collective-permute-start | bytes 393224 | tf_op jit(solution)/shard_map/ppermute | solution.py:250
  9.2 17.7 %collective-permute-start.7 = (bf16[256,256]{1,0:T(8,128)(2,1)S(1)}, bf16[256,256]{1,0:T(8,128)(2,1)S(1)}, u32[]{:S(2)}, u32[]{:S(2)}) collective-permute-start(bf16[256,256]{1,0:T(8,128)(2,1)S(1)} %collective-permute-done.3.refs_1_), channel_id=1, source_target_pairs={{0,4},{4,0},{8,12},{12,8},{16,20},{20,16},{24,28},{28,24},{1,5},{5... | collective-permute-start | bytes 393224 | tf_op jit(solution)/shard_map/ppermute | solution.py:209
  10.9 16.0 %collective-permute-start.6 = (bf16[256,256]{1,0:T(8,128)(2,1)S(1)}, bf16[256,256]{1,0:T(8,128)(2,1)S(1)}, u32[]{:S(2)}, u32[]{:S(2)}) collective-permute-start(bf16[256,256]{1,0:T(8,128)(2,1)S(1)} %collective-permute-done.refs_0_), channel_id=1, source_target_pairs={{0,4},{4,0},{8,12},{12,8},{16,20},{20,16},{24,28},{28,24},{1,5},{5... | collective-permute-start | bytes 393224 | tf_op jit(solution)/shard_map/ppermute | solution.py:209
  11.7 5.0 %collective-permute-start.1 = (bf16[256,256]{1,0:T(8,128)(2,1)S(1)}, bf16[256,256]{1,0:T(8,128)(2,1)S(1)}, u32[]{:S(2)}, u32[]{:S(2)}) collective-permute-start(bf16[256,256]{1,0:T(8,128)(2,1)S(1)} %collective-permute-done.refs_0_), channel_id=1, source_target_pairs={{0,8},{4,12},{8,16},{12,20},{16,24},{20,28},{24,0},{28,4},{1,9},{5... | collective-permute-start | bytes 393224 | tf_op jit(solution)/shard_map/ppermute | solution.py:250
  13.0 20.0 %collective-permute-start.5 = (bf16[256,256]{1,0:T(8,128)(2,1)S(1)}, bf16[256,256]{1,0:T(8,128)(2,1)S(1)}, u32[]{:S(2)}, u32[]{:S(2)}) collective-permute-start(bf16[256,256]{1,0:T(8,128)(2,1)S(1)} %broadcast_select_fusion), channel_id=1, source_target_pairs={{0,4},{4,0},{8,12},{12,8},{16,20},{20,16},{24,28},{28,24},{1,5},{5... | collective-permute-start | bytes 393224 | tf_op jit(solution)/shard_map/ppermute | solution.py:209
  16.7 16.2 %collective-permute-start.2 = (bf16[256,256]{1,0:T(8,128)(2,1)S(1)}, bf16[256,256]{1,0:T(8,128)(2,1)S(1)}, u32[]{:S(2)}, u32[]{:S(2)}) collective-permute-start(bf16[256,256]{1,0:T(8,128)(2,1)S(1)} %broadcast_select_fusion.1), channel_id=1, source_target_pairs={{0,4},{4,0},{8,12},{12,8},{16,20},{20,16},{24,28},{28,24},{1,5},{5... | collective-permute-start | bytes 393224 | tf_op jit(solution)/shard_map/ppermute | solution.py:209
  18.8 1.0 %copy-start = (bf16[256,1024]{1,0:T(8,128)(2,1)S(1)}, bf16[256,1024]{1,0:T(8,128)(2,1)}, u32[]{:S(2)}) copy-start(bf16[256,1024]{1,0:T(8,128)(2,1)} %q_ref.9) | copy-start | bytes 1572868
  22.8 1.0 %copy-start.1 = (bf16[256,1024]{1,0:T(8,128)(2,1)S(1)}, bf16[256,1024]{1,0:T(8,128)(2,1)}, u32[]{:S(2)}) copy-start(bf16[256,1024]{1,0:T(8,128)(2,1)} %q_ref.9) | copy-start | bytes 1572868
  38.6 3.0 %collective-permute-start.9 = (bf16[1,256,1024]{2,1,0:T(8,128)(2,1)S(1)}, bf16[1,256,1024]{2,1,0:T(8,128)(2,1)S(1)}, u32[]{:S(2)}, u32[]{:S(2)}) collective-permute-start(bf16[1,256,1024]{2,1,0:T(8,128)(2,1)S(1)} %p0.1), channel_id=1, source_target_pairs={{0,1},{1,0},{2,3},{3,2},{4,5},{5,4},{6,7},{7,6},{8,9},{9,8},{10,11... | collective-permute-start | bytes 1572872 | tf_op jit(solution)/shard_map/ppermute | solution.py:209
  41.1 4.5 %collective-permute-start.8 = (bf16[1,256,1024]{2,1,0:T(8,128)(2,1)S(1)}, bf16[1,256,1024]{2,1,0:T(8,128)(2,1)S(1)}, u32[]{:S(2)}, u32[]{:S(2)}) collective-permute-start(bf16[1,256,1024]{2,1,0:T(8,128)(2,1)S(1)} %p1.1), channel_id=1, source_target_pairs={{0,1},{1,0},{2,3},{3,2},{4,5},{5,4},{6,7},{7,6},{8,9},{9,8},{10,11... | collective-permute-start | bytes 1572872 | tf_op jit(solution)/shard_map/ppermute | solution.py:209
  43.9 13.9 %collective-permute-start.10 = (bf16[1,256,1024]{2,1,0:T(8,128)(2,1)S(1)}, bf16[1,256,1024]{2,1,0:T(8,128)(2,1)S(1)}, u32[]{:S(2)}, u32[]{:S(2)}) collective-permute-start(bf16[1,256,1024]{2,1,0:T(8,128)(2,1)S(1)} %p2.1), channel_id=1, source_target_pairs={{0,2},{1,3},{2,0},{3,1},{4,6},{5,7},{6,4},{7,5},{8,10},{9,11},{10,... | collective-permute-start | bytes 1572872 | tf_op jit(solution)/shard_map/ppermute | solution.py:209

commit v2 on v0

v2 whole, which is shorter than its diff:
```python
import jax
import jax.numpy as jnp
from jax import lax
from jax.experimental import pallas as pl
from jax.experimental.pallas import tpu as pltpu
from jax.sharding import PartitionSpec as P

HEAD_DIM = 128
REACH = 15
LOG2E = 1.4426950408889634
masked_score = -1e30
WEIGHT_COPIES = 8
VMEM_LIMIT = 20 * 1024 * 1024

vmem = pl.BlockSpec(memory_space=pltpu.VMEM)
smem = pl.BlockSpec(memory_space=pltpu.SMEM)
hbm = pl.BlockSpec(memory_space=pltpu.HBM)


def in_hbm(array):
    return pltpu.with_memory_space_constraint(array, pltpu.HBM)


def in_vmem(arrays):
    return [pltpu.with_memory_space_constraint(a, pltpu.VMEM) for a in arrays]


def params():
    return pltpu.CompilerParams(vmem_limit_bytes=VMEM_LIMIT)


def document_starts(offsets, first, rows):
    positions = first + lax.broadcasted_iota(jnp.int32, (1, rows), 1)
    starts = jnp.zeros((1, rows), jnp.int32)
    for i in range(1, offsets.shape[0] - 1):
        starts = jnp.where(positions >= offsets[i], offsets[i], starts)
    return starts


def scores_of(keys, query):
    return lax.dot_general(keys, query, (((1,), (1,)), ((), ())), preferred_element_type=jnp.float32)


def visible_keys(starts, key_start, rows, first):
    key_pos = key_start + lax.broadcasted_iota(jnp.int32, (rows, 1), 0)
    visible = key_pos >= starts
    if first is not None:
        visible = visible & (key_pos <= first + lax.broadcasted_iota(jnp.int32, (1, rows), 1))
    return visible


def score_block(q_ref, k_ref, visible, before):
    factor = HEAD_DIM ** -0.5 * LOG2E
    heads = q_ref.shape[1] // HEAD_DIM
    each = heads // (k_ref.shape[1] // HEAD_DIM)
    groups = [h // each for h in range(heads)]
    scores = [
        scores_of(k_ref[:, g * HEAD_DIM : (g + 1) * HEAD_DIM], q_ref[:, h * HEAD_DIM : (h + 1) * HEAD_DIM])
        for h, g in enumerate(groups)
    ]
    scores = [jnp.where(visible, s, masked_score) for s in scores]
    tops = [jnp.max(s, axis=0, keepdims=True) for s in scores]
    if before is not None:
        olds = [before[0][h : h + 1, :] for h in range(heads)]
        tops = [jnp.maximum(old, top) for old, top in zip(olds, tops)]
    weights = [jnp.exp2((s - top) * factor) for s, top in zip(scores, tops)]
    totals = [jnp.sum(w, axis=0, keepdims=True) for w in weights]
    weights = [w.astype(jnp.bfloat16) for w in weights]
    if before is None:
        return tops, totals, weights, None
    alphas = [jnp.exp2((old - top) * factor) for old, top in zip(olds, tops)]
    totals = [before[1][h : h + 1, :] * alphas[h] + totals[h] for h in range(heads)]
    return tops, totals, weights, alphas


def value_block(v_ref, weights, alphas, acc_ref):
    groups = v_ref.shape[1] // HEAD_DIM
    each = len(weights) // groups
    values = [v_ref[:, g * HEAD_DIM : (g + 1) * HEAD_DIM].T for g in range(groups)]
    sums = [jnp.dot(values[h // each], w, preferred_element_type=jnp.float32) for h, w in enumerate(weights)]
    if alphas is None:
        return sums
    return [acc_ref[h] * alphas[h] + s for h, s in enumerate(sums)]


def store_rows(ref, rows):
    for h, row in enumerate(rows):
        ref[h : h + 1, :] = row


def state_shapes(heads, rows):
    return [
        jax.ShapeDtypeStruct((heads, rows), jnp.float32),
        jax.ShapeDtypeStruct((heads, rows), jnp.float32),
        jax.ShapeDtypeStruct((heads, HEAD_DIM, rows), jnp.float32),
    ]


def first_row(rows):
    return lax.axis_index("ctx") * rows


def weight_shape(out_weight, count):
    return jax.ShapeDtypeStruct((out_weight.shape[0], out_weight.shape[1] // 4), out_weight.dtype)


def weight_copies(w_ref, parts, sems, far_core, far_next, count):
    depth = w_ref.shape[0]
    block = w_ref.shape[1] // count
    me = lax.axis_index("head")
    bits = (me % 2 + far_core) % 2 + 2 * ((me // 2 + far_next) % 2)
    pieces = sems.shape[0] // (count // 4)
    step = depth // pieces
    copies = []
    for i in range(count // 4):
        columns = pl.ds(pl.multiple_of((bits + 4 * i) * block, block), block)
        for j in range(pieces):
            rows = slice(j * step, (j + 1) * step)
            source = w_ref.at[rows, columns]
            target = parts.at[rows, i * block : (i + 1) * block]
            copies.append(pltpu.make_async_copy(source, target, sems.at[i * pieces + j]))
    return copies


def own_call(offsets, q, keys, values, out_weight, count):
    rows, width = q.shape

    def kernel(offsets_ref, q_in, k_in, v_in, w_in, starts_ref, q_ref, k_ref, v_ref, w_ref, top_ref, total_ref, acc_ref, sems, w_sems):
        copies = [
            pltpu.make_async_copy(source, target, sems.at[i])
            for i, (source, target) in enumerate(((k_in, k_ref), (q_in, q_ref), (v_in, v_ref)))
        ]
        weight = weight_copies(w_in, w_ref, w_sems, 1, 1, count)
        for copy in copies + weight:
            copy.start()
        first = first_row(rows)
        starts = document_starts(offsets_ref, first, rows)
        starts_ref[...] = starts
        visible = visible_keys(starts, first, rows, first)
        for copy in copies:
            copy.wait()
        tops, totals, weights, _ = score_block(q_ref, k_ref, visible, None)
        store_rows(top_ref, tops)
        store_rows(total_ref, totals)
        for h, out in enumerate(value_block(v_ref, weights, None, None)):
            acc_ref[h] = out
        for copy in weight:
            copy.wait()

    outs = pl.pallas_call(
        kernel,
        out_shape=[
            jax.ShapeDtypeStruct((1, rows), jnp.int32),
            *[jax.ShapeDtypeStruct(x.shape, x.dtype) for x in (q, keys, values)],
            weight_shape(out_weight, count),
            *state_shapes(width // HEAD_DIM, rows),
        ],
        in_specs=[smem] + [hbm] * 4,
        out_specs=[vmem] * 8,
        scratch_shapes=[pltpu.SemaphoreType.DMA((3,)), pltpu.SemaphoreType.DMA((count // 4 * WEIGHT_COPIES,))],
        compiler_params=params(),
        cost_estimate=cost(width, rows, 1),
        name="own",
    )(offsets, *[in_hbm(x) for x in (q, keys, values, out_weight)])
    return outs[:5], outs[5:]


def cost(width, rows, blocks):
    return pl.CostEstimate(flops=4 * width * rows * rows * blocks, bytes_accessed=0, transcendentals=width // HEAD_DIM * rows * rows * blocks)


def attend_call(starts, q, pieces, state, out_weight, kinds, count):
    rows, width = q.shape
    n = len(pieces)

    def kernel(starts_ref, q_ref, *refs):
        before, w_in = refs[2 * n : 2 * n + 3], refs[2 * n + 3]
        after, parts = refs[2 * n + 4 : 2 * n + 7], refs[2 * n + 7 : 2 * n + 7 + len(kinds)]
        sems = refs[-1]
        copies = []
        for i, (part, kind) in enumerate(zip(parts, kinds)):
            copies += weight_copies(w_in, part, sems.at[i], *kind, count)
        for copy in copies:
            copy.start()
        for i, (_, _, back) in enumerate(pieces):
            k_ref, v_ref = refs[2 * i : 2 * i + 2]
            position = lax.axis_index("ctx")
            key_start = (position - back(lax.rem(position, 2))) * rows
            visible = visible_keys(starts_ref[...], key_start, rows, None)
            source = before if i == 0 else after
            tops, totals, weights, alphas = score_block(q_ref, k_ref, visible, source)
            store_rows(after[0], tops)
            store_rows(after[1], totals)
            for h, out in enumerate(value_block(v_ref, weights, alphas, source[2])):
                after[2][h] = out
        for copy in copies:
            copy.wait()

    first = 2 + 2 * n
    outs = pl.pallas_call(
        kernel,
        out_shape=[*state_shapes(width // HEAD_DIM, rows), *[weight_shape(out_weight, count)] * len(kinds)],
        in_specs=[vmem] * (first + 3) + [hbm],
        out_specs=[vmem] * (3 + len(kinds)),
        scratch_shapes=[pltpu.SemaphoreType.DMA((max(len(kinds), 1), count // 4 * WEIGHT_COPIES))],
        input_output_aliases={first + i: i for i in range(3)},
        compiler_params=params(),
        cost_estimate=cost(width, rows, n),
        name="attend",
    )(*in_vmem([starts, q, *[a for p in pieces for a in p[:2]], *state]), in_hbm(out_weight))
    return outs[:3], outs[3:]


def last_scores_call(starts, q, keys, back, state):
    rows, width = q.shape
    heads = width // HEAD_DIM

    def kernel(starts_ref, q_ref, k_ref, top_ref, old_total_ref, total_ref, alpha_ref, weights_ref):
        position = lax.axis_index("ctx")
        key_start = (position - back(lax.rem(position, 2))) * rows
        visible = visible_keys(starts_ref[...], key_start, rows, None)
        _, totals, weights, alphas = score_block(q_ref, k_ref, visible, (top_ref, old_total_ref))
        store_rows(total_ref, totals)
        store_rows(alpha_ref, alphas)
        for h, w in enumerate(weights):
            weights_ref[h] = w

    return pl.pallas_call(
        kernel,
        out_shape=[
            jax.ShapeDtypeStruct((heads, rows), jnp.float32),
            jax.ShapeDtypeStruct((heads, rows), jnp.float32),
            jax.ShapeDtypeStruct((heads, rows, rows), jnp.bfloat16),
        ],
        in_specs=[vmem] * 5,
        out_specs=[vmem] * 3,
        compiler_params=params(),
        cost_estimate=cost(width, rows, 1),
        name="last_scores",
    )(*in_vmem([starts, q, keys, state[0], state[1]]))


def project_into(out_ref, att_ref, w_ref, added_ref):
    block = out_ref.shape[2]
    step = min(block, 256)
    for i in range(out_ref.shape[0]):
        for start in range(0, block, step):
            cut = slice(start, start + step)
            columns = w_ref[:, i * block + start : i * block + start + step]
            value = jnp.dot(att_ref[...], columns, preferred_element_type=jnp.float32)
            if added_ref is not None:
                value = value + added_ref[i, :, cut].astype(jnp.float32)
            out_ref[i, :, cut] = value.astype(out_ref.dtype)


def finish_call(values, weights, totals, alphas, acc, w_far, count):
    heads, _, rows = acc.shape
    block = w_far.shape[1] * 4 // count

    def kernel(v_ref, p_ref, total_ref, alpha_ref, acc_ref, w_ref, att_ref, far_ref):
        scales = [alpha_ref[h : h + 1, :] for h in range(heads)]
        outs = value_block(v_ref, [p_ref[h] for h in range(heads)], scales, acc_ref)
        for h, out in enumerate(outs):
            head = out * (1.0 / total_ref[h : h + 1, :])
            att_ref[:, h * HEAD_DIM : (h + 1) * HEAD_DIM] = head.T.astype(jnp.bfloat16)
        project_into(far_ref, att_ref, w_ref, None)

    return pl.pallas_call(
        kernel,
        out_shape=[
            jax.ShapeDtypeStruct((rows, heads * HEAD_DIM), jnp.bfloat16),
            jax.ShapeDtypeStruct((count // 4, rows, block), jnp.bfloat16),
        ],
        in_specs=[vmem] * 6,
        out_specs=[vmem] * 2,
        compiler_params=params(),
        name="finish",
    )(*in_vmem([values, weights, totals, alphas, acc, w_far]))


def project_call(attended, weight, added, count, out_type, name):
    rows, depth = attended.shape
    block = weight.shape[1] * 4 // count

    def kernel(att_ref, w_ref, *refs):
        project_into(refs[-1], att_ref, w_ref, refs[0] if len(refs) > 1 else None)

    more = [] if added is None else [added]
    return pl.pallas_call(
        kernel,
        out_shape=jax.ShapeDtypeStruct((count // 4, rows, block), out_type),
        in_specs=[vmem] * (2 + len(more)),
        out_specs=vmem,
        compiler_params=params(),
        cost_estimate=pl.CostEstimate(flops=2 * rows * depth * weight.shape[1], bytes_accessed=0, transcendentals=0),
        name=name,
    )(*in_vmem([attended, weight, *more]))


def kept_call(attended, out_weight, added, count):
    rows, depth = attended.shape
    part = weight_shape(out_weight, count)

    def kernel(att_ref, w_in, added_ref, out_ref, w_ref, sems):
        copies = weight_copies(w_in, w_ref, sems, 0, 0, count)
        for copy in copies:
            copy.start()
        for copy in copies:
            copy.wait()
        project_into(out_ref, att_ref, w_ref, added_ref)

    return pl.pallas_call(
        kernel,
        out_shape=jax.ShapeDtypeStruct(added.shape, jnp.float32),
        in_specs=[vmem, hbm, vmem],
        out_specs=vmem,
        scratch_shapes=[pltpu.VMEM(part.shape, part.dtype), pltpu.SemaphoreType.DMA((count // 4 * WEIGHT_COPIES,))],
        compiler_params=params(),
        cost_estimate=pl.CostEstimate(flops=2 * rows * depth * part.shape[1], bytes_accessed=0, transcendentals=0),
        name="kept",
    )(*in_vmem([attended]), in_hbm(out_weight), *in_vmem([added]))


def pick_call(moving, own):
    def kernel(moving_ref, own_ref, out_ref):
        odd = lax.rem(lax.axis_index("ctx"), 2) == 1

        @pl.when(odd)
        def _():
            out_ref[...] = moving_ref[...]

        @pl.when(jnp.logical_not(odd))
        def _():
            out_ref[...] = own_ref[...]

    return pl.pallas_call(
        kernel,
        out_shape=jax.ShapeDtypeStruct(own.shape, own.dtype),
        in_specs=[vmem] * 2,
        out_specs=vmem,
        compiler_params=params(),
        name="pick",
    )(*in_vmem([moving, own]))


def output_call(kept, arrived):
    rows, block = kept.shape

    def kernel(kept_ref, arrived_ref, out_ref):
        out_ref[...] = (kept_ref[...] + arrived_ref[...].astype(jnp.float32)).T.astype(jnp.bfloat16)

    return pl.pallas_call(
        kernel,
        out_shape=jax.ShapeDtypeStruct((block, rows), jnp.bfloat16),
        in_specs=[vmem] * 2,
        out_specs=vmem,
        compiler_params=params(),
        name="output",
    )(kept, arrived)


def swapped(array, axis, bit):
    return lax.ppermute(array, axis, [(i, i ^ bit) for i in range(lax.axis_size(axis))])


def summed_over_heads(attended, far, weights, out_weight, count):
    w_near, w_sent = weights
    got_far = swapped(far, "head", 1)
    near = project_call(attended, w_near, None, count, jnp.bfloat16, "near")
    got_near = swapped(near, "head", 1)
    sent = project_call(attended, w_sent, got_far, count, jnp.bfloat16, "sent")
    got = swapped(sent, "head", 2)
    kept = kept_call(attended, out_weight, got_near, count)
    me = lax.axis_index("head")
    for b in range(2, count.bit_length() - 1):
        kept = kept + got.astype(jnp.float32)
        pairs = kept.reshape(kept.shape[0] // 2, 2, *kept.shape[1:])
        bit = (me >> b) & 1
        sent = lax.dynamic_index_in_dim(pairs, 1 - bit, 1, keepdims=False)
        kept = lax.dynamic_index_in_dim(pairs, bit, 1, keepdims=False)
        got = swapped(sent.astype(jnp.bfloat16), "head", 1 << b)
    return output_call(kept[0], got[0])


def on_device(queries, key_vectors, value_vectors, out_weight, offsets):
    devices = lax.axis_size("ctx")
    heads = lax.axis_size("head")
    pair_steps = (min(REACH, devices // 2) + 1) // 2

    def shifted(block):
        return lax.ppermute(block, "ctx", [(i, (i + 2) % devices) for i in range(devices)])

    moving = (key_vectors, value_vectors)
    (starts, q, keys, values, w_far), state = own_call(offsets, queries, key_vectors, value_vectors, out_weight, heads)
    waiting, brought = [], []
    for step in range(1, pair_steps + 1):
        moving = tuple(shifted(m) for m in moving)
        first, state = lax.optimization_barrier((moving[0], state))
        moving = (first, moving[1])
        waiting.append((*moving, lambda x, step=step: 2 * step))
        if step < pair_steps:
            across = tuple(swapped(m, "ctx", 1) for m in moving)
            kinds = [(1, 0)] if step == 1 else []
            state, more = attend_call(starts, q, waiting, state, out_weight, kinds, heads)
            brought += [*more]
            waiting = [(*across, lambda x, step=step: 2 * step - 1 + 2 * x)]
    across = tuple(swapped(pick_call(m, o), "ctx", 1) for m, o in zip(moving, (keys, values)))
    kinds = [(0, 1)] if brought else [(1, 0), (0, 1)]
    state, more = attend_call(starts, q, waiting, state, out_weight, kinds, heads)

    def back(x):
        return jnp.where(x == 1, 1, 2 * pair_steps - 1)

    totals, alphas, weights = last_scores_call(starts, q, across[0], back, state)
    attended, far = finish_call(across[1], weights, totals, alphas, state[2], w_far, heads)
    return summed_over_heads(attended, far, brought + [*more], out_weight, heads)


def solution(mesh):
    placed = (P("ctx", "head"), P("ctx", "head"), P("ctx", "head"), P("head", None), P())
    return jax.shard_map(
        on_device, mesh=mesh, in_specs=placed, out_specs=P("head", "ctx"), check_vma=False
    )
```

time: 159 us -> 44.4 us (0.28)
  waiting for transfers between devices: 62.6 us -> 14.2 us
  starting transfers between devices: 34.8 us -> 12.8 us
  matrix products: 20.8 us -> 0 us
  local copies, waits for them, and re-layouts: 19.5 us -> 0.65 us
  Pallas kernels: 0 us -> 16.3 us
  between operations: 13.5 us -> 0.1 us
  other arithmetic: 6.65 us -> 0 us
    reduce_scatter x1 -> x0, waiting for transfers between devices: 35.6 us -> none  [on_device(): lax.psum_scatter(lax.dot_general(out_weight, attended, (((0,), (1,)), (()...]
    ppermute x7 -> x11, starting transfers between devices: 34.8 us -> 12.8 us  [the longest x7 7.52 us: swapped(): lax.ppermute(array, axis, [(i, i ^ bit) for i in range(lax.axis_size(axis...]
    dot_general x17 -> x0, matrix products: 20.8 us -> none  [the longest x8 9.39 us: attend(): jnp.einsum('avmk,kab->mavb', attention_probs.astype(jnp.bfloat16), value_...]
    pallas_call x0 -> x11, Pallas kernels: none -> 16.3 us  [the longest x2 6.34 us: attend_call(): pl.pallas_call(kernel, out_shape=[*state_shapes(width // HEAD_DIM, rows),...]
    ppermute x7 -> x11, waiting for transfers between devices: 26.9 us -> 14.2 us  [the longest x7 10.8 us: swapped(): lax.ppermute(array, axis, [(i, i ^ bit) for i in range(lax.axis_size(axis...]
    while x43 -> x0, local copies, waits for them, and re-layouts: 9.06 us -> none
    reduce_sum x16 -> x0, other arithmetic: 4.89 us -> none  [the longest x8 4.19 us: attend(): row_sum = row_sum * rescale + jnp.sum(attention_probs, axis=-1)]
    unnamed x10 -> x2, local copies, waits for them, and re-layouts: 4.52 us -> 0.65 us
  transfers between devices with their start and end apart: 8 -> 11, of which waited for: 8 -> 5; matrix products, arithmetic and copies ran while one was open for 2% -> 0% of each run, Pallas kernels for 0% -> 32%
where the time goes in v2:
time: 44.4 us; the launch traced here: 44.2 us
  Pallas kernels  16.3 us (37%)
  waiting for transfers between devices  14.2 us (32%)
  starting transfers between devices  12.8 us (29%)
  local copies, waits for them, and re-layouts  0.65 us (1%)
    ppermute x7, waiting for transfers between devices, swapped(): lax.ppermute(array, axis, [(i, i ^ bit) for i in range(lax.axis_size(axis...  10.8 us
    ppermute x7, starting transfers between devices, swapped(): lax.ppermute(array, axis, [(i, i ^ bit) for i in range(lax.axis_size(axis...  7.52 us
    pallas_call x2, Pallas kernels, attend_call(): pl.pallas_call(kernel, out_shape=[*state_shapes(width // HEAD_DIM, rows),...  6.34 us
    ppermute x4, starting transfers between devices, shifted(): lax.ppermute(block, 'ctx', [(i, (i + 2) % devices) for i in range(devices)])  5.31 us
    ppermute x4, waiting for transfers between devices, shifted(): lax.ppermute(block, 'ctx', [(i, (i + 2) % devices) for i in range(devices)])  3.45 us
    pallas_call x1, Pallas kernels, own_call(): pl.pallas_call(kernel, out_shape=[jax.ShapeDtypeStruct((1, rows), jnp.int...  3.39 us
    pallas_call x1, Pallas kernels, kept_call(): pl.pallas_call(kernel, out_shape=jax.ShapeDtypeStruct(added.shape, jnp.fl...  2.29 us
    pallas_call x2, Pallas kernels, project_call(): pl.pallas_call(kernel, out_shape=jax.ShapeDtypeStruct((count // 4, rows,...  1.41 us
  transfers between devices with their start and end apart: 11, of which 5 were waited for; matrix products, arithmetic and copies ran while one was open for 0% of the time, Pallas kernels for 32%

profile of v2, /device:TPU:0, one launch (start us, length us, event | category | flops | bytes accessed | tf_op | source)
XLA Modules:
  0.0 44.2 jit_solution(15540790563905177584)
XLA Ops:
  0.0 3.0 %collective-permute-start.3 = (bf16[256,256]{1,0:T(8,128)(2,1)}, bf16[256,256]{1,0:T(8,128)(2,1)S(1)}, u32[]{:S(2)}, u32[]{:S(2)}) collective-permute-start(bf16[256,256]{1,0:T(8,128)(2,1)} %k_in.1), channel_id=1, source_target_pairs={{0,8},{4,12},{8,16},{12,20},{16,24},{20,28},{24,0},{28,4},{1,9},{5... | collective-permute-start | bytes 393224 | tf_op jit(solution)/shard_map/ppermute | solution.py:391
  3.0 1.6 %collective-permute-start = (bf16[256,256]{1,0:T(8,128)(2,1)}, bf16[256,256]{1,0:T(8,128)(2,1)S(1)}, u32[]{:S(2)}, u32[]{:S(2)}) collective-permute-start(bf16[256,256]{1,0:T(8,128)(2,1)} %v_in.1), channel_id=1, source_target_pairs={{0,8},{4,12},{8,16},{12,20},{16,24},{20,28},{24,0},{28,4},{1,9},{5... | collective-permute-start | bytes 393224 | tf_op jit(solution)/shard_map/ppermute | solution.py:391
  4.6 0.0 copy-start
  4.6 0.7 %copy-done = s32[5]{0:T(128)S(1)} copy-done((s32[5]{0:T(128)S(1)}, s32[5]{0:T(128)}, u32[]{:S(2)}) %copy-start) | copy-done | bytes 44
  5.3 3.4 %own.1 = (s32[1,256]{1,0:T(1,128)S(1)}, bf16[256,1024]{1,0:T(8,128)(2,1)S(1)}, bf16[256,256]{1,0:T(8,128)(2,1)S(1)}, bf16[256,256]{1,0:T(8,128)(2,1)S(1)}, bf16[...) custom-call(s32[5]{0:T(128)S(1)} %copy-done, ...), custom_call_target="tpu_custom_call" | custom-call | flops 268435456 | tf_op jit(solution)/shard_map/own/pallas_call | solution.py:150
  8.7 0.9 %collective-permute-done.3.refs_0_ = bf16[256,256]{1,0:T(8,128)(2,1)S(1)} collective-permute-done((bf16[256,256]{1,0:T(8,128)(2,1)}, bf16[256,256]{1,0:T(8,128)(2,1)S(1)}, u32[]{:S(2)}, u32[]{:S(2)}) %collective-permute-start.3) | collective-permute-done | bytes 131104 | tf_op jit(solution)/shard_map/ppermute | solution.py:391
  9.6 0.7 %collective-permute-start.4 = (bf16[256,256]{1,0:T(8,128)(2,1)S(1)}, bf16[256,256]{1,0:T(8,128)(2,1)S(1)}, u32[]{:S(2)}, u32[]{:S(2)}) collective-permute-start(bf16[256,256]{1,0:T(8,128)(2,1)S(1)} %collective-permute-done.3.refs_0_), channel_id=1, source_target_pairs={{0,8},{4,12},{8,16},{12,20},{16,24},{20,28},{24,0},{28,4},{1,9},{5... | collective-permute-start | bytes 393224 | tf_op jit(solution)/shard_map/ppermute | solution.py:391
  10.3 1.3 %collective-permute-done.refs_1_ = bf16[256,256]{1,0:T(8,128)(2,1)S(1)} collective-permute-done((bf16[256,256]{1,0:T(8,128)(2,1)}, bf16[256,256]{1,0:T(8,128)(2,1)S(1)}, u32[]{:S(2)}, u32[]{:S(2)}) %collective-permute-start) | collective-permute-done | bytes 131104 | tf_op jit(solution)/shard_map/ppermute | solution.py:391
  11.6 0.0 collective-permute-start.1
  11.6 1.5 %collective-permute-start.7 = (bf16[256,256]{1,0:T(8,128)(2,1)S(1)}, bf16[256,256]{1,0:T(8,128)(2,1)S(1)}, u32[]{:S(2)}, u32[]{:S(2)}) collective-permute-start(bf16[256,256]{1,0:T(8,128)(2,1)S(1)} %collective-permute-done.refs_1_), channel_id=1, source_target_pairs={{0,4},{4,0},{8,12},{12,8},{16,20},{20,16},{24,28},{28,24},{1,5},{5... | collective-permute-start | bytes 393224 | tf_op jit(solution)/shard_map/ppermute | solution.py:363
  13.1 0.5 %collective-permute-start.6 = (bf16[256,256]{1,0:T(8,128)(2,1)S(1)}, bf16[256,256]{1,0:T(8,128)(2,1)S(1)}, u32[]{:S(2)}, u32[]{:S(2)}) collective-permute-start(bf16[256,256]{1,0:T(8,128)(2,1)S(1)} %collective-permute-done.3.refs_0_), channel_id=1, source_target_pairs={{0,4},{4,0},{8,12},{12,8},{16,20},{20,16},{24,28},{28,24},{1,5},{5... | collective-permute-start | bytes 393224 | tf_op jit(solution)/shard_map/ppermute | solution.py:363
  13.6 2.6 %attend.2 = (f32[8,256]{1,0:T(8,128)S(1)}, f32[8,256]{1,0:T(8,128)S(1)}, f32[8,128,256]{2,1,0:T(8,128)S(1)}, bf16[1024,1024]{1,0:T(8,128)(2,1)S(1)}) custom-call(s32[1,256]{1,0:T(1,128)S(1)} %get-tuple-element.35.starts_ref, bf16[256,1024]{1,0:T(8,128)(2,1)S(1)} %get-tuple-element.36.q_ref, ...), custom_call_target="tpu_custom_call", output_to_operand_aliasing={{0}: (4, {}), {1}: (5, {}), {2}: (6, {})} | custom-call | flops 268435456 | tf_op jit(solution)/shard_map/attend/pallas_call | solution.py:200
  16.2 1.2 %collective-permute-done.4.moving_ref.refs_2_ = bf16[256,256]{1,0:T(8,128)(2,1)S(1)} collective-permute-done((bf16[256,256]{1,0:T(8,128)(2,1)S(1)}, bf16[256,256]{1,0:T(8,128)(2,1)S(1)}, u32[]{:S(2)}, u32[]{:S(2)}) %collective-permute-start.4) | collective-permute-done | bytes 131104 | tf_op jit(solution)/shard_map/ppermute | solution.py:391
  17.5 1.9 %collective-permute-start.5 = (bf16[256,256]{1,0:T(8,128)(2,1)S(1)}, bf16[256,256]{1,0:T(8,128)(2,1)S(1)}, u32[]{:S(2)}, u32[]{:S(2)}) collective-permute-start(bf16[256,256]{1,0:T(8,128)(2,1)S(1)} %pick.3), channel_id=1, source_target_pairs={{0,4},{4,0},{8,12},{12,8},{16,20},{20,16},{24,28},{28,24},{1,5},{5... | collective-permute-start | bytes 393224 | tf_op jit(solution)/shard_map/ppermute | solution.py:363
  19.4 0.0 collective-permute-done.1.moving_ref.refs_3_
  19.4 1.4 %collective-permute-start.2 = (bf16[256,256]{1,0:T(8,128)(2,1)S(1)}, bf16[256,256]{1,0:T(8,128)(2,1)S(1)}, u32[]{:S(2)}, u32[]{:S(2)}) collective-permute-start(bf16[256,256]{1,0:T(8,128)(2,1)S(1)} %pick.2), channel_id=1, source_target_pairs={{0,4},{4,0},{8,12},{12,8},{16,20},{20,16},{24,28},{28,24},{1,5},{5... | collective-permute-start | bytes 393224 | tf_op jit(solution)/shard_map/ppermute | solution.py:363
  20.8 0.0 collective-permute-done.7.refs_1_
  20.8 0.0 collective-permute-done.6.refs_0_
  20.8 3.7 %attend.3 = (f32[8,256]{1,0:T(8,128)S(1)}, f32[8,256]{1,0:T(8,128)S(1)}, f32[8,128,256]{2,1,0:T(8,128)S(1)}, bf16[1024,1024]{1,0:T(8,128)(2,1)S(1)}) custom-call(s32[1,256]{1,0:T(1,128)S(1)} %get-tuple-element.35.starts_ref, bf16[256,1024]{1,0:T(8,128)(2,1)S(1)} %get-tuple-element.36.q_ref, ...), custom_call_target="tpu_custom_call", output_to_operand_aliasing={{0}: (6, {}), {1}: (7, {}), {2}: (8, {})} | custom-call | flops 536870912 | tf_op jit(solution)/shard_map/attend/pallas_call | solution.py:200
  24.5 0.0 collective-permute-done.5.k_ref
  24.5 0.9 %last_scores.1 = (f32[8,256]{1,0:T(8,128)S(1)}, f32[8,256]{1,0:T(8,128)S(1)}, bf16[8,256,256]{2,1,0:T(8,128)(2,1)S(1)}) custom-call(s32[1,256]{1,0:T(1,128)S(1)} %get-tuple-element.35.starts_ref, bf16[256,1024]{1,0:T(8,128)(2,1)S(1)} %get-tuple-element.36.q_ref, bf16[256,256]{1,0:T(8,128)(2,1)S(1)} %collective-permute-done.5.k_ref, ...), custom_call_target="tpu_custom_call" | custom-call | flops 268435456 | tf_op jit(solution)/shard_map/last_scores/pallas_call | solution.py:228
  25.4 0.0 collective-permute-done.2.v_ref
  25.4 1.0 %finish.1 = (bf16[256,1024]{1,0:T(8,128)(2,1)S(1)}, bf16[1,256,1024]{2,1,0:T(8,128)(2,1)S(1)}) custom-call(bf16[256,256]{1,0:T(8,128)(2,1)S(1)} %collective-permute-done.2.v_ref, bf16[8,256,256]{2,1,0:T(8,128)(2,1)S(1)} %get-tuple-element.54.p_ref, f32[8,256]{1,0:T(8,128)S(1)} %get-tuple-element.55.total_ref, f32[8,256]{1,0:T(8,128)S(1)} %get-tuple-element.56.alpha_ref, ...), custom_call_target="tpu_custom_call" | custom-call | tf_op jit(solution)/shard_map/finish/pallas_call | solution.py:268
  26.4 0.1 collective-permute-start.9
  26.5 0.7 %near.1 = bf16[1,256,1024]{2,1,0:T(8,128)(2,1)S(1)} custom-call(bf16[256,1024]{1,0:T(8,128)(2,1)S(1)} %get-tuple-element.59.att_ref, bf16[1024,1024]{1,0:T(8,128)(2,1)S(1)} %get-tuple-element.60.w_ref), custom_call_target="tpu_custom_call" | custom-call | flops 536870912 | tf_op jit(solution)/shard_map/near/pallas_call | solution.py:289
  27.2 0.6 %collective-permute-start.8 = (bf16[1,256,1024]{2,1,0:T(8,128)(2,1)S(1)}, bf16[1,256,1024]{2,1,0:T(8,128)(2,1)S(1)}, u32[]{:S(2)}, u32[]{:S(2)}) collective-permute-start(bf16[1,256,1024]{2,1,0:T(8,128)(2,1)S(1)} %near.1), channel_id=1, source_target_pairs={{0,1},{1,0},{2,3},{3,2},{4,5},{5,4},{6,7},{7,6},{8,9},{9,8},{10,11... | collective-permute-start | bytes 1572872 | tf_op jit(solution)/shard_map/ppermute | solution.py:363
  27.8 0.6 %collective-permute-done.9.refs_0_ = bf16[1,256,1024]{2,1,0:T(8,128)(2,1)S(1)} collective-permute-done((bf16[1,256,1024]{2,1,0:T(8,128)(2,1)S(1)}, bf16[1,256,1024]{2,1,0:T(8,128)(2,1)S(1)}, u32[]{:S(2)}, u32[]{:S(2)}) %collective-permute-start.9) | collective-permute-done | bytes 524320 | tf_op jit(solution)/shard_map/ppermute | solution.py:363
  28.4 0.7 %sent.1 = bf16[1,256,1024]{2,1,0:T(8,128)(2,1)S(1)} custom-call(bf16[256,1024]{1,0:T(8,128)(2,1)S(1)} %get-tuple-element.59.att_ref, bf16[1024,1024]{1,0:T(8,128)(2,1)S(1)} %get-tuple-element.61.w_ref, bf16[1,256,1024]{2,1,0:T(8,128)(2,1)S(1)} %collective-permute-done.9.refs_0_), custom_call_target="tpu_custom_call" | custom-call | flops 536870912 | tf_op jit(solution)/shard_map/sent/pallas_call | solution.py:289
  29.1 1.6 %collective-permute-start.10 = (bf16[1,256,1024]{2,1,0:T(8,128)(2,1)S(1)}, bf16[1,256,1024]{2,1,0:T(8,128)(2,1)S(1)}, u32[]{:S(2)}, u32[]{:S(2)}) collective-permute-start(bf16[1,256,1024]{2,1,0:T(8,128)(2,1)S(1)} %sent.1), channel_id=1, source_target_pairs={{0,2},{1,3},{2,0},{3,1},{4,6},{5,7},{6,4},{7,5},{8,10},{9,11},{10,... | collective-permute-start | bytes 1572872 | tf_op jit(solution)/shard_map/ppermute | solution.py:363
  30.7 0.0 collective-permute-done.8.added_ref
  30.7 2.3 %kept.1 = f32[1,256,1024]{2,1,0:T(8,128)S(1)} custom-call(bf16[256,1024]{1,0:T(8,128)(2,1)S(1)} %get-tuple-element.59.att_ref, bf16[1024,4096]{1,0:T(8,128)(2,1)} %w_in.3, bf16[1,256,1024]{2,1,0:T(8,128)(2,1)S(1)} %collective-permute-done.8.added_ref), custom_call_target="tpu_custom_call" | custom-call | flops 536870912 | tf_op jit(solution)/shard_map/kept/pallas_call | solution.py:312
  33.0 10.2 %collective-permute-done.10 = bf16[1,256,1024]{2,1,0:T(8,128)(2,1)S(1)} collective-permute-done((bf16[1,256,1024]{2,1,0:T(8,128)(2,1)S(1)}, bf16[1,256,1024]{2,1,0:T(8,128)(2,1)S(1)}, u32[]{:S(2)}, u32[]{:S(2)}) %collective-permute-start.10) | collective-permute-done | bytes 524320 | tf_op jit(solution)/shard_map/ppermute | solution.py:363
  43.2 1.0 %output.1 = bf16[1024,256]{1,0:T(8,128)(2,1)} custom-call(f32[256,1024]{1,0:T(8,128)S(1)} %bitcast.2, bf16[256,1024]{1,0:T(8,128)(2,1)S(1)} %bitcast.3), custom_call_target="tpu_custom_call" | custom-call | tf_op jit(solution)/shard_map/output/pallas_call | solution.py:352
  (2 shorter events, 0.0 us)
Async XLA Ops:
  0.0 9.6 %collective-permute-start.3 = (bf16[256,256]{1,0:T(8,128)(2,1)}, bf16[256,256]{1,0:T(8,128)(2,1)S(1)}, u32[]{:S(2)}, u32[]{:S(2)}) collective-permute-start(bf16[256,256]{1,0:T(8,128)(2,1)} %k_in.1), channel_id=1, source_target_pairs={{0,8},{4,12},{8,16},{12,20},{16,24},{20,28},{24,0},{28,4},{1,9},{5... | collective-permute-start | bytes 393224 | tf_op jit(solution)/shard_map/ppermute | solution.py:391
  3.0 8.5 %collective-permute-start = (bf16[256,256]{1,0:T(8,128)(2,1)}, bf16[256,256]{1,0:T(8,128)(2,1)S(1)}, u32[]{:S(2)}, u32[]{:S(2)}) collective-permute-start(bf16[256,256]{1,0:T(8,128)(2,1)} %v_in.1), channel_id=1, source_target_pairs={{0,8},{4,12},{8,16},{12,20},{16,24},{20,28},{24,0},{28,4},{1,9},{5... | collective-permute-start | bytes 393224 | tf_op jit(solution)/shard_map/ppermute | solution.py:391
  4.6 0.7 %copy-start = (s32[5]{0:T(128)S(1)}, s32[5]{0:T(128)}, u32[]{:S(2)}) copy-start(s32[5]{0:T(128)} %offsets_ref.1) | copy-start | bytes 64
  9.6 7.9 %collective-permute-start.4 = (bf16[256,256]{1,0:T(8,128)(2,1)S(1)}, bf16[256,256]{1,0:T(8,128)(2,1)S(1)}, u32[]{:S(2)}, u32[]{:S(2)}) collective-permute-start(bf16[256,256]{1,0:T(8,128)(2,1)S(1)} %collective-permute-done.3.refs_0_), channel_id=1, source_target_pairs={{0,8},{4,12},{8,16},{12,20},{16,24},{20,28},{24,0},{28,4},{1,9},{5... | collective-permute-start | bytes 393224 | tf_op jit(solution)/shard_map/ppermute | solution.py:391
  11.6 7.8 %collective-permute-start.1 = (bf16[256,256]{1,0:T(8,128)(2,1)S(1)}, bf16[256,256]{1,0:T(8,128)(2,1)S(1)}, u32[]{:S(2)}, u32[]{:S(2)}) collective-permute-start(bf16[256,256]{1,0:T(8,128)(2,1)S(1)} %collective-permute-done.refs_1_), channel_id=1, source_target_pairs={{0,8},{4,12},{8,16},{12,20},{16,24},{20,28},{24,0},{28,4},{1,9},{5... | collective-permute-start | bytes 393224 | tf_op jit(solution)/shard_map/ppermute | solution.py:391
  11.6 9.2 %collective-permute-start.7 = (bf16[256,256]{1,0:T(8,128)(2,1)S(1)}, bf16[256,256]{1,0:T(8,128)(2,1)S(1)}, u32[]{:S(2)}, u32[]{:S(2)}) collective-permute-start(bf16[256,256]{1,0:T(8,128)(2,1)S(1)} %collective-permute-done.refs_1_), channel_id=1, source_target_pairs={{0,4},{4,0},{8,12},{12,8},{16,20},{20,16},{24,28},{28,24},{1,5},{5... | collective-permute-start | bytes 393224 | tf_op jit(solution)/shard_map/ppermute | solution.py:363
  13.1 7.7 %collective-permute-start.6 = (bf16[256,256]{1,0:T(8,128)(2,1)S(1)}, bf16[256,256]{1,0:T(8,128)(2,1)S(1)}, u32[]{:S(2)}, u32[]{:S(2)}) collective-permute-start(bf16[256,256]{1,0:T(8,128)(2,1)S(1)} %collective-permute-done.3.refs_0_), channel_id=1, source_target_pairs={{0,4},{4,0},{8,12},{12,8},{16,20},{20,16},{24,28},{28,24},{1,5},{5... | collective-permute-start | bytes 393224 | tf_op jit(solution)/shard_map/ppermute | solution.py:363
  17.5 7.1 %collective-permute-start.5 = (bf16[256,256]{1,0:T(8,128)(2,1)S(1)}, bf16[256,256]{1,0:T(8,128)(2,1)S(1)}, u32[]{:S(2)}, u32[]{:S(2)}) collective-permute-start(bf16[256,256]{1,0:T(8,128)(2,1)S(1)} %pick.3), channel_id=1, source_target_pairs={{0,4},{4,0},{8,12},{12,8},{16,20},{20,16},{24,28},{28,24},{1,5},{5... | collective-permute-start | bytes 393224 | tf_op jit(solution)/shard_map/ppermute | solution.py:363
  19.4 6.0 %collective-permute-start.2 = (bf16[256,256]{1,0:T(8,128)(2,1)S(1)}, bf16[256,256]{1,0:T(8,128)(2,1)S(1)}, u32[]{:S(2)}, u32[]{:S(2)}) collective-permute-start(bf16[256,256]{1,0:T(8,128)(2,1)S(1)} %pick.2), channel_id=1, source_target_pairs={{0,4},{4,0},{8,12},{12,8},{16,20},{20,16},{24,28},{28,24},{1,5},{5... | collective-permute-start | bytes 393224 | tf_op jit(solution)/shard_map/ppermute | solution.py:363
  26.4 2.0 %collective-permute-start.9 = (bf16[1,256,1024]{2,1,0:T(8,128)(2,1)S(1)}, bf16[1,256,1024]{2,1,0:T(8,128)(2,1)S(1)}, u32[]{:S(2)}, u32[]{:S(2)}) collective-permute-start(bf16[1,256,1024]{2,1,0:T(8,128)(2,1)S(1)} %get-tuple-element.62), channel_id=1, source_target_pairs={{0,1},{1,0},{2,3},{3,2},{4,5},{5,4},{6,7},{7,6},{8,9},{9,8},{10,11... | collective-permute-start | bytes 1572872 | tf_op jit(solution)/shard_map/ppermute | solution.py:363
  27.2 3.5 %collective-permute-start.8 = (bf16[1,256,1024]{2,1,0:T(8,128)(2,1)S(1)}, bf16[1,256,1024]{2,1,0:T(8,128)(2,1)S(1)}, u32[]{:S(2)}, u32[]{:S(2)}) collective-permute-start(bf16[1,256,1024]{2,1,0:T(8,128)(2,1)S(1)} %near.1), channel_id=1, source_target_pairs={{0,1},{1,0},{2,3},{3,2},{4,5},{5,4},{6,7},{7,6},{8,9},{9,8},{10,11... | collective-permute-start | bytes 1572872 | tf_op jit(solution)/shard_map/ppermute | solution.py:363
  29.1 14.0 %collective-permute-start.10 = (bf16[1,256,1024]{2,1,0:T(8,128)(2,1)S(1)}, bf16[1,256,1024]{2,1,0:T(8,128)(2,1)S(1)}, u32[]{:S(2)}, u32[]{:S(2)}) collective-permute-start(bf16[1,256,1024]{2,1,0:T(8,128)(2,1)S(1)} %sent.1), channel_id=1, source_target_pairs={{0,2},{1,3},{2,0},{3,1},{4,6},{5,7},{6,4},{7,5},{8,10},{9,11},{10,... | collective-permute-start | bytes 1572872 | tf_op jit(solution)/shard_map/ppermute | solution.py:363
